TPU v7x, 768 devices: a whole 4x8x12 slice. The times are simulated.
768 devices in a mesh: aa: 96 (over z, x, core), ba: 8 (over y).
Axes of the slice: x: 4, y: 8, z: 12, core: 2. Of those that a mesh axis runs over, the one named last changes fastest.
Arguments:
- prev_vector: float32 [4608, 6144], P('aa', 'ba'), may hold values from -6 to 6
- this_vector: float32 [4608, 6144], P('aa', 'ba'), may hold values from -6 to 6
- diagonal: float32 [4608, 6144], P('aa', 'ba'), may hold values from -0.5 to 0.5
- alpha_blocks: bfloat16 [36, 2, 128, 128], replicated, may hold values from -0.21875 to 0.21875
- alpha_classes: int32 [8], replicated, may hold values from 1 to 8, 36 in all
- alpha_offsets: int32 [36, 2], replicated, may hold values from 0 to 7
- alpha_mask: int32 [36, 2], replicated, may hold values 0 or 1
- beta_blocks: bfloat16 [48, 2, 128, 128], replicated, may hold values from -0.21875 to 0.21875
- beta_classes: int32 [8], replicated, may hold values from 1 to 10, 48 in all
- beta_offsets: int32 [48, 2], replicated, may hold values from 0 to 9
- beta_mask: int32 [48, 2], replicated, may hold values 0 or 1
Outputs:
- next_vector: float32 [4608, 6144], P('aa', 'ba')
- after_vector: float32 [4608, 6144], P('aa', 'ba')
Inputs may be any that keep to these rules, and one draw needn't show every extreme that they name: `alpha_classes`: alpha strings are ordered by class; the class sizes sum to 36 blocks and one class has exactly 8 blocks. `beta_classes`: beta strings are ordered by class; the class sizes sum to 48 blocks and one class has exactly 10 blocks.
All inputs are finite; a program needn't handle non-finite values.
Results may differ from a plain program's by a relative error of at most 0.0065.
Values may be sent and summed in bfloat16 or wider, within the bound.
A program may use at most 64 MiB of HBM per device.

v0:
```python
import jax
import jax.numpy as jnp
from jax import lax
from jax.sharding import Mesh
from jax.sharding import PartitionSpec as P

STEPS = 2
AA = ("aa_0", "aa_1", "aa_2")


def in_blocks(value, dim, devices):
    before, after = (value.shape[:dim], value.shape[dim + 1 :])
    return jnp.moveaxis(value.reshape(*before, devices, -1, *after), dim, 0)


def in_order(parts, dim):
    parts = jnp.moveaxis(parts, 0, dim)
    dims = parts.shape
    return parts.reshape(*dims[:dim], dims[dim] * dims[dim + 1], *dims[dim + 2 :])


def turned_blocks(parts, axes, turns):
    dims = [lax.axis_size(a) for a in axes]
    parts = parts.reshape(*dims, *parts.shape[1:])
    for k in turns:
        parts = lax.all_to_all(parts, axes[k], split_axis=k, concat_axis=k, tiled=True)
    return parts.reshape(-1, *parts.shape[len(axes) :])


def exchange_by_chip(value, groups, turns, split_dim, concat_dim):
    devices = lax.axis_size(groups[0]) * lax.axis_size(groups[1])
    parts = in_blocks(value, split_dim, devices)
    return in_order(turned_blocks(parts, groups, turns), concat_dim)


def sent_to_all(value, axis):
    devices = lax.axis_size(axis)
    return lax.all_to_all(
        jnp.broadcast_to(value[None], (devices, *value.shape)), axis, 0, 0, tiled=True
    )


def gathered_copies(value, axis, dim):
    parts = sent_to_all(value, axis)
    return in_order(parts, dim)


def block_columns(class_sizes, offsets):
    class_ends = jnp.cumsum(class_sizes)
    class_starts = class_ends - class_sizes
    row_ids = jnp.arange(offsets.shape[0], dtype=jnp.int32)[:, None]
    inside = (row_ids >= class_starts[None, :]) & (row_ids < class_ends[None, :])
    first_block = jnp.sum(jnp.where(inside, class_starts[None, :], 0), axis=1)
    class_length = jnp.sum(jnp.where(inside, class_sizes[None, :], 0), axis=1)
    return first_block[:, None] + offsets % class_length[:, None]


def couple_last(pieces, blocks, columns, live_mask):
    out_blocks, slot_count, block_size, _ = blocks.shape
    item_count = pieces.shape[0]
    stacked = pieces.reshape(item_count, -1, block_size)
    picked = stacked[:, columns, :] * live_mask[None, :, :, None]
    result = jnp.einsum("crkj,rkij->cri", picked, blocks, preferred_element_type=jnp.float32)
    return result.reshape(item_count, out_blocks * block_size).astype(jnp.bfloat16)


def on_device(
    prev_vector,
    this_vector,
    diagonal,
    alpha_blocks,
    alpha_classes,
    alpha_offsets,
    alpha_mask,
    beta_blocks,
    beta_classes,
    beta_offsets,
    beta_mask,
):
    alpha_cols = block_columns(alpha_classes, alpha_offsets)
    alpha_live = alpha_mask.astype(jnp.bfloat16)
    beta_cols = block_columns(beta_classes, beta_offsets)
    beta_live = beta_mask.astype(jnp.bfloat16)
    alpha_count = lax.axis_size(AA)
    beta_count = lax.axis_size("ba")
    own_alpha, own_beta = prev_vector.shape
    own_count = beta_blocks.shape[0] // beta_count
    first_own = lax.axis_index("ba") * own_count
    own_blocks = lax.dynamic_slice_in_dim(beta_blocks, first_own, own_count, 0)
    own_cols = lax.dynamic_slice_in_dim(beta_cols, first_own, own_count, 0)
    own_live = lax.dynamic_slice_in_dim(beta_live, first_own, own_count, 0)
    previous = prev_vector
    current = this_vector
    produced = []
    for iteration in range(STEPS):
        rounded = current.astype(jnp.bfloat16)
        alpha_shaped = rounded.reshape(own_alpha, alpha_count, own_beta // alpha_count)
        pieces = lax.all_to_all(alpha_shaped, AA, split_axis=1, concat_axis=0, tiled=True)
        whole_alpha, single, columns_here = pieces.shape
        flat = pieces.reshape(whole_alpha, columns_here)
        applied = couple_last(flat.T, alpha_blocks, alpha_cols, alpha_live).T
        alpha_local = applied.reshape(whole_alpha, single, columns_here)
        alpha_back = exchange_by_chip(alpha_local, (("aa_0", "aa_1"), "aa_2"), (1, 0), 0, 1)
        alpha_term = alpha_back.reshape(own_alpha, own_beta)
        whole_rows = gathered_copies(rounded, "ba", 1)
        beta_term = couple_last(whole_rows, own_blocks, own_cols, own_live)
        newer = (
            2.0
            * (alpha_term.astype(jnp.float32) + beta_term.astype(jnp.float32) + diagonal * current)
            - previous
        )
        previous = current
        current = newer
        produced.append(newer)
    return (produced[0], produced[-1])


def solution(mesh):
    finer = Mesh(mesh.devices.reshape(12, 4, 2, mesh.shape["ba"]), ("aa_0", "aa_1", "aa_2", "ba"))
    return jax.shard_map(
        on_device,
        mesh=finer,
        in_specs=(P(AA, "ba"), P(AA, "ba"), P(AA, "ba"), P(), P(), P(), P(), P(), P(), P(), P()),
        out_specs=(P(AA, "ba"), P(AA, "ba")),
        check_vma=False,
    )
```

profile of v0, /device:TPU:8, one launch (start us, length us, event | category | flops | bytes accessed | tf_op | source)
XLA Modules:
  0.0 179.8 jit_solution(1253000437591730737)
XLA Ops:
  0.6 1.1 convert_element_type.82
  3.4 19.2 %all-to-all-start = ((bf16[96,2,192]{2,1,0:T(2,128)(2,1)}), bf16[96,2,192]{2,1,0:T(2,128)(2,1)S(1)}, u32[]{:S(2)}, u32[]{:S(2)}) async-start(bf16[96,2,192]{2,1,0:T(2,128)(2,1)} %reshape.182), calls=%async_computation | async-start | bytes 196608 | tf_op jit(solution)/shard_map/all_to_all | solution.py:98
  25.7 1.4 reduce-window.17
  28.0 7.8 %all-to-all-done = bf16[96,2,192]{2,1,0:T(2,128)(2,1)S(1)} async-done(((bf16[96,2,192]{2,1,0:T(2,128)(2,1)}), bf16[96,2,192]{2,1,0:T(2,128)(2,1)S(1)}, u32[]{:S(2)}, u32[]{:S(2)}) %all-to-all-start) | async-done | bytes 73760 | tf_op jit(solution)/shard_map/all_to_all | solution.py:98
  36.9 2.4 %fusion.7 = bf16[4608,8]{0,1:T(8,128)(2,1)S(1)} fusion(bf16[36,2,128,128]{3,2,1,0:T(8,128)(2,1)} %param.14, bf16[36,2,8,128]{3,2,1,0:T(8,128)(2,1)S(1)} %bitcast.172, bf16[36,2]{1,0:T(8,128)(2,1)S(1)} %copy.128), kind=kOutput, calls=%fused_computation.15 | convolution fusion | flops 18984960 | bytes 2580624 | tf_op jit(solution)/shard_map/crkj,rkij->cri/dot_general | solution.py:63
  39.9 3.8 %all_to_all.60 = bf16[2,2,9216]{2,1,0:T(2,128)(2,1)S(1)} all-to-all(bf16[2,2,9216]{2,1,0:T(2,128)(2,1)S(1)} %reshape.184), channel_id=1, replica_groups=mesh['aa_0'=12,'aa_1'=4,'aa_2'=2,'ba'=8] {'aa_2'}, dimensions={0} | all-to-all | bytes 147456 | tf_op jit(solution)/shard_map/all_to_all | solution.py:26
  44.1 0.9 reshape.186
  45.0 4.5 %all-to-all-start.2 = ((bf16[48,2,384]{2,1,0:T(2,128)(2,1)}), bf16[48,2,384]{2,1,0:T(2,128)(2,1)S(1)}, u32[]{:S(2)}, u32[]{:S(2)}) async-start(bf16[48,2,384]{2,1,0:T(2,128)(2,1)} %reshape.186), calls=%async_computation.2 | async-start | bytes 147456 | tf_op jit(solution)/shard_map/all_to_all | solution.py:26
  51.0 11.4 %all-to-all-done.2 = bf16[48,2,384]{2,1,0:T(2,128)(2,1)S(1)} async-done(((bf16[48,2,384]{2,1,0:T(2,128)(2,1)}), bf16[48,2,384]{2,1,0:T(2,128)(2,1)S(1)}, u32[]{:S(2)}, u32[]{:S(2)}) %all-to-all-start.2) | async-done | bytes 73760 | tf_op jit(solution)/shard_map/all_to_all | solution.py:26
  62.3 1.7 broadcast_in_dim.82
  64.1 7.5 %all-to-all-start.3 = ((bf16[8,48,768]{2,1,0:T(8,128)(2,1)}), bf16[8,48,768]{2,1,0:T(8,128)(2,1)}, u32[]{:S(2)}, u32[]{:S(2)}) async-start(bf16[8,48,768]{2,1,0:T(8,128)(2,1)} %broadcast_in_dim.82), calls=%async_computation.3 | async-start | bytes 1179648 | tf_op jit(solution)/shard_map/all_to_all | solution.py:38
  75.8 12.0 %all-to-all-done.3 = bf16[8,48,768]{2,1,0:T(8,128)(2,1)} async-done(((bf16[8,48,768]{2,1,0:T(8,128)(2,1)}), bf16[8,48,768]{2,1,0:T(8,128)(2,1)}, u32[]{:S(2)}, u32[]{:S(2)}) %all-to-all-start.3) | async-done | bytes 589856 | tf_op jit(solution)/shard_map/all_to_all | solution.py:38
  87.8 2.0 %copy.132 = bf16[48,8,768]{2,1,0:T(8,128)(2,1)} copy(bf16[48,8,768]{2,0,1:T(8,128)(2,1)} %bitcast.17) | data formatting | bytes 1179648 | tf_op jit(solution)/shard_map/transpose | solution.py:17
  89.8 2.3 %reshape_reshape.8 = bf16[48,48,128]{2,1,0:T(8,128)(2,1)} reshape(bf16[48,8,768]{2,1,0:T(8,128)(2,1)} %copy.132) | data formatting | bytes 1179648 | tf_op jit(solution)/shard_map/reshape;reshape | solution.py:61
  92.2 2.0 %copy.134 = bf16[48,48,128]{2,0,1:T(8,128)(2,1)} copy(bf16[48,48,128]{2,1,0:T(8,128)(2,1)} %reshape_reshape.8) | data formatting | bytes 1179648 | tf_op jit(solution)/shard_map/reshape;reshape | solution.py:61
  94.2 1.6 gather_fusion.1
  95.8 1.0 fusion.5
  96.8 1.8 fusion.36
  98.6 1.0 copy.138
  99.9 19.1 %all_to_all.61 = bf16[96,2,192]{2,1,0:T(2,128)(2,1)S(1)} all-to-all(bf16[96,2,192]{2,1,0:T(2,128)(2,1)S(1)} %reshape.188), channel_id=1, replica_groups=mesh['aa_0'=12,'aa_1'=4,'aa_2'=2,'ba'=8] {'aa_0','aa_1','aa_2'}, dimensions={0} | all-to-all | bytes 147456 | tf_op jit(solution)/shard_map/all_to_all | solution.py:98
  120.2 2.4 %fusion.9 = bf16[4608,8]{0,1:T(8,128)(2,1)S(1)} fusion(bf16[36,2,128,128]{3,2,1,0:T(8,128)(2,1)} %param.14, bf16[36,2,8,128]{3,2,1,0:T(8,128)(2,1)S(1)} %bitcast.171, bf16[36,2]{1,0:T(8,128)(2,1)S(1)} %copy.128), kind=kOutput, calls=%fused_computation.17 | convolution fusion | flops 18984960 | bytes 2580624 | tf_op jit(solution)/shard_map/crkj,rkij->cri/dot_general | solution.py:63
  123.1 3.8 %all_to_all.62 = bf16[2,2,9216]{2,1,0:T(2,128)(2,1)S(1)} all-to-all(bf16[2,2,9216]{2,1,0:T(2,128)(2,1)S(1)} %reshape.190), channel_id=1, replica_groups=mesh['aa_0'=12,'aa_1'=4,'aa_2'=2,'ba'=8] {'aa_2'}, dimensions={0} | all-to-all | bytes 147456 | tf_op jit(solution)/shard_map/all_to_all | solution.py:26
  127.6 17.1 %all_to_all.63 = bf16[48,2,384]{2,1,0:T(2,128)(2,1)S(1)} all-to-all(bf16[48,2,384]{2,1,0:T(2,128)(2,1)S(1)} %reshape.192), channel_id=1, replica_groups=mesh['aa_0'=12,'aa_1'=4,'aa_2'=2,'ba'=8] {'aa_0','aa_1'}, dimensions={0} | all-to-all | bytes 147456 | tf_op jit(solution)/shard_map/all_to_all | solution.py:26
  144.7 1.7 broadcast_in_dim.87
  146.4 5.5 %all-to-all-start.7 = ((bf16[8,48,768]{2,1,0:T(8,128)(2,1)}), bf16[8,48,768]{2,1,0:T(8,128)(2,1)}, u32[]{:S(2)}, u32[]{:S(2)}) async-start(bf16[8,48,768]{2,1,0:T(8,128)(2,1)} %broadcast_in_dim.87), calls=%async_computation.7 | async-start | bytes 1179648 | tf_op jit(solution)/shard_map/all_to_all | solution.py:38
  153.0 15.2 %all-to-all-done.7 = bf16[8,48,768]{2,1,0:T(8,128)(2,1)} async-done(((bf16[8,48,768]{2,1,0:T(8,128)(2,1)}), bf16[8,48,768]{2,1,0:T(8,128)(2,1)}, u32[]{:S(2)}, u32[]{:S(2)}) %all-to-all-start.7) | async-done | bytes 589856 | tf_op jit(solution)/shard_map/all_to_all | solution.py:38
  168.2 2.0 %copy.143 = bf16[48,8,768]{2,1,0:T(8,128)(2,1)} copy(bf16[48,8,768]{2,0,1:T(8,128)(2,1)} %bitcast.40) | data formatting | bytes 1179648 | tf_op jit(solution)/shard_map/transpose | solution.py:17
  170.2 2.4 %reshape_reshape.9 = bf16[48,48,128]{2,1,0:T(8,128)(2,1)} reshape(bf16[48,8,768]{2,1,0:T(8,128)(2,1)} %copy.143) | data formatting | bytes 1179648 | tf_op jit(solution)/shard_map/reshape;reshape | solution.py:61
  172.6 2.0 %copy.144 = bf16[48,48,128]{2,0,1:T(8,128)(2,1)} copy(bf16[48,48,128]{2,1,0:T(8,128)(2,1)} %reshape_reshape.9) | data formatting | bytes 1179648 | tf_op jit(solution)/shard_map/reshape;reshape | solution.py:61
  174.6 2.3 %gather_fusion.3 = bf16[12,48,128]{2,1,0:T(8,128)(2,1)} fusion(bf16[48,48,128]{2,0,1:T(8,128)(2,1)} %copy.144, s32[1024]{0:T(1024)S(1)} %copy-done.6), kind=kCustom, calls=%fused_computation.3 | custom fusion | bytes 294960 | tf_op jit(solution)/shard_map/gather | solution.py:62
  176.9 1.2 fusion.3
  178.1 1.7 fusion.14
  (73 shorter events, 17.0 us)
Async XLA Ops:
  0.6 95.2 %copy-start = (bf16[48,2,128,128]{3,2,1,0:T(8,128)(2,1)S(1)}, bf16[48,2,128,128]{3,2,1,0:T(8,128)(2,1)}, u32[]{:S(2)}) copy-start(bf16[48,2,128,128]{3,2,1,0:T(8,128)(2,1)} %param.18) | copy-start | bytes 9437188
  1.7 0.6 copy-start.3
  3.4 32.4 %all-to-all-start = ((bf16[96,2,192]{2,1,0:T(2,128)(2,1)}), bf16[96,2,192]{2,1,0:T(2,128)(2,1)S(1)}, u32[]{:S(2)}, u32[]{:S(2)}) async-start(bf16[96,2,192]{2,1,0:T(2,128)(2,1)} %reshape.182), calls=%async_computation | async-start | bytes 196608 | tf_op jit(solution)/shard_map/all_to_all | solution.py:98
  45.0 17.3 %all-to-all-start.2 = ((bf16[48,2,384]{2,1,0:T(2,128)(2,1)}), bf16[48,2,384]{2,1,0:T(2,128)(2,1)S(1)}, u32[]{:S(2)}, u32[]{:S(2)}) async-start(bf16[48,2,384]{2,1,0:T(2,128)(2,1)} %reshape.186), calls=%async_computation.2 | async-start | bytes 147456 | tf_op jit(solution)/shard_map/all_to_all | solution.py:26
  64.1 23.7 %all-to-all-start.3 = ((bf16[8,48,768]{2,1,0:T(8,128)(2,1)}), bf16[8,48,768]{2,1,0:T(8,128)(2,1)}, u32[]{:S(2)}, u32[]{:S(2)}) async-start(bf16[8,48,768]{2,1,0:T(8,128)(2,1)} %broadcast_in_dim.82), calls=%async_computation.3 | async-start | bytes 1179648 | tf_op jit(solution)/shard_map/all_to_all | solution.py:38
  75.8 18.4 %copy-start.5 = (s32[1024]{0:T(1024)S(1)}, s32[1024]{0:T(1024)}, u32[]{:S(2)}) copy-start(s32[1024]{0:T(1024)} %pad_clamp_fusion) | copy-start | bytes 12292
  75.8 21.0 %copy-start.1 = (f32[48,768]{1,0:T(8,128)S(1)}, f32[48,768]{1,0:T(8,128)}, u32[]{:S(2)}) copy-start(f32[48,768]{1,0:T(8,128)} %param.12) | copy-start | bytes 442372
  146.4 21.8 %all-to-all-start.7 = ((bf16[8,48,768]{2,1,0:T(8,128)(2,1)}), bf16[8,48,768]{2,1,0:T(8,128)(2,1)}, u32[]{:S(2)}, u32[]{:S(2)}) async-start(bf16[8,48,768]{2,1,0:T(8,128)(2,1)} %broadcast_in_dim.87), calls=%async_computation.7 | async-start | bytes 1179648 | tf_op jit(solution)/shard_map/all_to_all | solution.py:38
  152.2 22.5 %copy-start.6 = (s32[1024]{0:T(1024)S(1)}, s32[1024]{0:T(1024)}, u32[]{:S(2)}) copy-start(s32[1024]{0:T(1024)} %pad_clamp_fusion) | copy-start | bytes 12292
  152.2 24.8 %copy-start.7 = (bf16[6,2]{1,0:T(8,128)(2,1)S(1)}, bf16[6,2]{1,0:T(8,128)(2,1)}, u32[]{:S(2)}) copy-start(bf16[6,2]{1,0:T(8,128)(2,1)} %copy.135) | copy-start | bytes 76
  153.0 25.1 %copy-start.2 = (f32[48,768]{1,0:T(8,128)S(1)}, f32[48,768]{1,0:T(8,128)}, u32[]{:S(2)}) copy-start(f32[48,768]{1,0:T(8,128)} %param.12) | copy-start | bytes 442372
  153.0 25.1 %copy-start.4 = (f32[48,768]{1,0:T(8,128)S(1)}, f32[48,768]{1,0:T(8,128)}, u32[]{:S(2)}) copy-start(f32[48,768]{1,0:T(8,128)} %copy.146) | copy-start | bytes 442372
where the time goes:
time: 181 us; the launch traced here: 180 us
  waiting for transfers between devices  46.2 us (26%)
  blocking collectives  43.7 us (24%)
  starting transfers between devices  36.8 us (20%)
  local copies, waits for them, and re-layouts  31.8 us (18%)
  other arithmetic  13.3 us (7%)
  matrix products  6.96 us (4%)
    all_to_all x2, waiting for transfers between devices, sent_to_all(): lax.all_to_all(jnp.broadcast_to(value[None], (devices, *value.shape)), ax...  27.1 us
    all_to_all x3, blocking collectives, turned_blocks(): lax.all_to_all(parts, axes[k], split_axis=k, concat_axis=k, tiled=True)  24.6 us
    all_to_all x1, starting transfers between devices, on_device(): lax.all_to_all(alpha_shaped, AA, split_axis=1, concat_axis=0, tiled=True)  19.2 us
    all_to_all x1, blocking collectives, on_device(): lax.all_to_all(alpha_shaped, AA, split_axis=1, concat_axis=0, tiled=True)  19.1 us
    all_to_all x2, starting transfers between devices, sent_to_all(): lax.all_to_all(jnp.broadcast_to(value[None], (devices, *value.shape)), ax...  13.1 us
    all_to_all x1, waiting for transfers between devices, turned_blocks(): lax.all_to_all(parts, axes[k], split_axis=k, concat_axis=k, tiled=True)  11.4 us
    another operation x4, local copies, waits for them, and re-layouts, couple_last(): stacked = pieces.reshape(item_count, -1, block_size)  8.74 us
    all_to_all x1, waiting for transfers between devices, on_device(): lax.all_to_all(alpha_shaped, AA, split_axis=1, concat_axis=0, tiled=True)  7.78 us
  transfers between devices with their start and end apart: 4, of which 4 were waited for; matrix products, arithmetic and copies ran while one was open for 7% of the time, Pallas kernels for 0%

commit v1 on v0

v1 whole, which is shorter than its diff:
```python
import jax
import jax.numpy as jnp
from jax import lax
from jax.experimental import pallas as pl
from jax.experimental.pallas import tpu as pltpu
from jax.sharding import PartitionSpec as P

BLK = 128
PLANES = 12
PLANE = 8
LINE = 8
ROWS = 48
COLB = 6
ROWB = 3
WIN = 10
TILE = 16
TILES = 3
PIECES = 27
YWIN = 24
NCLS = 8
MESH = pl.DeviceIdType.MESH


def remote(src, dst, send, recv, to):
    return pltpu.make_async_remote_copy(
        src_ref=src, dst_ref=dst, send_sem=send, recv_sem=recv, device_id=to, device_id_type=MESH
    )


def await_bytes(ref, sem):
    pltpu.make_async_copy(ref, ref, sem).wait()


def class_table(sizes):
    starts, lengths, first = [], [], jnp.int32(0)
    for c in range(NCLS):
        starts.append(first)
        lengths.append(sizes[c])
        first = first + sizes[c]
    return starts, lengths


def class_of(block, table):
    starts, lengths = table
    start, length = starts[0], lengths[0]
    for c in range(1, NCLS):
        later = block >= starts[c]
        start = jnp.where(later, starts[c], start)
        length = jnp.where(later, lengths[c], length)
    return start, length


def column_of(start, length, offset, halvings):
    for k in reversed(range(halvings)):
        step = length * (1 << k)
        offset = jnp.where(offset >= step, offset - step, offset)
    return start + offset


def kernel(
    prev_hbm, this_hbm, diag_hbm, ablk_hbm, acls, aoff, amask, bblk_hbm, bcls, boff, bmask,
    next_hbm, after_hbm,
    xv, pv, dv, tv, nv, ov, yw0, yw1, tb, win0, wint, win1, al0, al1, rec0, rec1, araw, braw, aw, bw,
    load_sem, store_sem, in_send, in_recv, out_send, out_recv, y_sem, self_sem,
):
    aa = lax.axis_index("aa")
    y = lax.axis_index("ba")
    z = lax.div(aa, PLANE)
    p = lax.rem(aa, PLANE)
    plane = {d: lax.rem(z + d + PLANES, PLANES) for d in (-2, -1, 0, 1, 2)}
    first = {d: plane[d] * PLANE for d in plane}
    line = {d: lax.rem(y + d + LINE, LINE) for d in (-2, -1, 1, 2)}
    is_home = p < COLB
    reaches = p < ROWB

    def at(d, q):
        return {"aa": first[d] + q, "ba": y}

    def along(d):
        return {"aa": aa, "ba": line[d]}

    loads = [pltpu.make_async_copy(this_hbm, xv, load_sem.at[0])]
    loads[0].start()

    barrier = pltpu.get_barrier_semaphore()

    def greet(to):
        pl.semaphore_signal(barrier, inc=1, device_id=to, device_id_type=MESH)

    for d in (-2, -1, 1, 2):
        greet(along(d))
    for d in (-1, 1):
        for q in range(PLANE):
            greet(at(d, q))
    for q in range(1, PLANE):
        greet(at(0, lax.rem(p + q, PLANE)))

    @pl.when(reaches)
    def _():
        for q in range(COLB):
            greet(at(-2, q))

    @pl.when(is_home)
    def _():
        for q in range(ROWB):
            greet(at(2, q))

    loads += [
        pltpu.make_async_copy(diag_hbm, dv, load_sem.at[1]),
        pltpu.make_async_copy(prev_hbm, pv, load_sem.at[2]),
        pltpu.make_async_copy(bblk_hbm.at[pl.ds(y * COLB, COLB)], braw, load_sem.at[3]),
    ]
    for k, (d, count) in enumerate(((-1, ROWB), (0, ROWB), (1, ROWB), (2, 1))):
        loads.append(
            pltpu.make_async_copy(
                ablk_hbm.at[pl.ds(plane[d] * ROWB, count)],
                araw.at[pl.ds(ROWB * k, count)],
                load_sem.at[4 + k],
            )
        )
    for c in loads[1:]:
        c.start()

    loads[0].wait()
    for cb in range(COLB):
        yw0[9 + cb] = xv[:, cb * BLK : (cb + 1) * BLK].astype(jnp.bfloat16).reshape(TILES, TILE, BLK)

    pl.semaphore_wait(barrier, 27 + jnp.where(reaches, COLB, 0) + jnp.where(is_home, ROWB, 0))

    def y_copies(w, step):
        parts = ((9, 6, 3, 1), (9, 6, 15, -1), (12, 3, 0, 2), (9, 3, 21, -2))
        return [
            remote(
                w.at[pl.ds(src, n)], w.at[pl.ds(dst, n)],
                y_sem.at[step, 0, k], y_sem.at[step, 1, k], along(d),
            )
            for k, (src, n, dst, d) in enumerate(parts)
        ]

    def piece(k):
        return pl.ds(TILES * k, TILES)

    def send_in(src, w, step):
        @pl.when(reaches)
        def _():
            for cb in range(COLB):
                remote(
                    src(cb), w.at[piece(3 * PLANE + p)],
                    in_send.at[step, 0], in_recv.at[step], at(-2, cb),
                ).start()

        for d, base in ((-1, 2 * PLANE), (1, 0)):
            for cb in range(COLB):
                remote(
                    src(cb), w.at[piece(base + p)], in_send.at[step, 1], in_recv.at[step], at(d, cb)
                ).start()
        for cb in range(COLB):

            @pl.when(p != cb)
            def _(cb=cb):
                remote(
                    src(cb), w.at[piece(PLANE + p)],
                    in_send.at[step, 2], in_recv.at[step], at(0, cb),
                ).start()

            @pl.when(p == cb)
            def _(cb=cb):
                pltpu.make_async_copy(
                    src(cb), w.at[piece(PLANE + p)], self_sem.at[step]
                ).start()

    def sent_in(step):
        @pl.when(reaches)
        def _():
            await_bytes(win0.at[pl.ds(0, COLB * TILES)], in_send.at[step, 0])

        await_bytes(win0.at[pl.ds(0, 2 * COLB * TILES)], in_send.at[step, 1])

        @pl.when(is_home)
        def _():
            await_bytes(win0.at[pl.ds(0, (COLB - 1) * TILES)], in_send.at[step, 2])

        @pl.when(jnp.logical_not(is_home))
        def _():
            await_bytes(win0.at[pl.ds(0, COLB * TILES)], in_send.at[step, 2])

    def arrived_in(w, step):
        await_bytes(w.at[pl.ds(0, (PIECES - 1) * TILES)], in_recv.at[step])
        await_bytes(w.at[pl.ds(0, TILES)], self_sem.at[step])

    def send_out(src, rec, step):
        for q in range(ROWB):
            remote(
                src.at[piece(3 * PLANE + q)], rec.at[3, p],
                out_send.at[step], out_recv.at[step, 1], at(2, q),
            ).start()
        for d, base, slot in ((1, 2 * PLANE, 0), (-1, 0, 2)):
            for q in range(PLANE):
                remote(
                    src.at[piece(base + q)], rec.at[slot, p],
                    out_send.at[step], out_recv.at[step, 0], at(d, q),
                ).start()
        for k in range(1, PLANE):
            q = lax.rem(p + k, PLANE)
            remote(
                src.at[piece(PLANE + q)], rec.at[1, p],
                out_send.at[step], out_recv.at[step, 0], at(0, q),
            ).start()
        pltpu.make_async_copy(
            src.at[piece(PLANE + p)], rec.at[1, p], self_sem.at[2 + step]
        ).start()

    def arrived_out(rec, step):
        @pl.when(reaches)
        def _():
            await_bytes(rec.at[3], out_recv.at[step, 1])

        @pl.when(is_home)
        def _():
            await_bytes(win0.at[pl.ds(0, (3 * COLB - 1) * TILES)], out_recv.at[step, 0])
            await_bytes(rec.at[3, 0], self_sem.at[2 + step])

        @pl.when(jnp.logical_not(is_home))
        def _():
            await_bytes(win0.at[pl.ds(0, 3 * COLB * TILES)], out_recv.at[step, 0])

    ys0 = y_copies(yw0, 0)
    for c in ys0:
        c.start()
    send_in(lambda cb: yw0.at[9 + cb], win0, 0)

    a_table = class_table(acls)
    b_table = class_table(bcls)
    a_at = []
    for j in range(WIN):
        block = lax.rem(z * ROWB - ROWB + j + PLANES * ROWB, PLANES * ROWB)
        start, length = class_of(block, a_table)
        a_at.append(
            [
                jnp.clip(
                    column_of(start, length, aoff[k, block], 3) - (z - 1) * ROWB, 0, WIN - 1
                )
                for k in range(2)
            ]
        )
    b_at = []
    for r in range(COLB):
        block = y * COLB + r
        start, length = class_of(block, b_table)
        b_at.append(
            [
                jnp.clip(
                    column_of(start, length, boff[k, block], 4) - y * COLB + 9, 0, YWIN - 1
                )
                for k in range(2)
            ]
        )
    slot_at = []
    for q in range(3):
        start, length = class_of(z * ROWB + lax.div(3 * p + q, PLANE), a_table)
        middle = start + lax.div(length - 1, 2)
        away = lax.div(middle, ROWB) - z
        slot_at.append(jnp.clip(jnp.where(away == -2, 3, away + 1), 0, 3))

    for c in loads[1:]:
        c.wait()
    for r in range(COLB):
        for k in range(2):
            live = bmask[k, y * COLB + r].astype(jnp.float32)
            bw[r, :, k * BLK : (k + 1) * BLK] = (braw[r, k].astype(jnp.float32) * live).astype(
                jnp.bfloat16
            )

    @pl.when(is_home)
    def _():
        for j in range(WIN):
            block = lax.rem(z * ROWB - ROWB + j + PLANES * ROWB, PLANES * ROWB)
            for k in range(2):
                live = amask[k, block].astype(jnp.float32)
                aw[j, :, k * BLK : (k + 1) * BLK] = (
                    araw[j, k].astype(jnp.float32) * live
                ).astype(jnp.bfloat16)
        al0[8 * WIN] = jnp.zeros((TILE, BLK), jnp.bfloat16)
        al1[8 * WIN] = jnp.zeros((TILE, BLK), jnp.bfloat16)

    def beta(w, r):
        both = jnp.concatenate([w[b_at[r][k]].reshape(ROWS, BLK) for k in range(2)], axis=1)
        out = lax.dot_general(
            both, bw[r], (((1,), (1,)), ((), ())), preferred_element_type=jnp.float32
        )
        return out.astype(jnp.bfloat16).astype(jnp.float32)

    def alpha(w, out):
        for j in range(WIN):
            both = jnp.concatenate(
                [w[pl.ds(a_at[j][k] * 8, 8)].reshape(BLK, BLK) for k in range(2)], axis=0
            )
            product = jnp.dot(aw[j], both, preferred_element_type=jnp.float32)
            out[8 * j : 8 * (j + 1)] = product.astype(jnp.bfloat16).reshape(8, TILE, BLK)

    def returned(rec, cb):
        return jnp.concatenate(
            [rec[slot_at[q], cb, q] for q in range(TILES)], axis=0
        ).astype(jnp.float32)

    for c in ys0:
        c.wait_recv()
    for cb in range(COLB):
        cols = slice(cb * BLK, (cb + 1) * BLK)
        t = 2.0 * (beta(yw0, cb) + dv[:, cols] * xv[:, cols]) - pv[:, cols]
        tv[:, cols] = t
        tb[cb] = t.astype(jnp.bfloat16).reshape(TILES, TILE, BLK)
    send_in(lambda cb: tb.at[cb], wint, 1)

    @pl.when(is_home)
    def _():
        arrived_in(win0, 0)
        alpha(win0, al0)
        send_out(al0, rec0, 0)
        arrived_in(wint, 1)
        for j in range(WIN):
            rows = slice(8 * j, 8 * (j + 1))
            win1[rows] = (
                2.0 * al0[rows].astype(jnp.float32) + wint[rows].astype(jnp.float32)
            ).astype(jnp.bfloat16)
        alpha(win1, al1)
        send_out(al1, rec1, 1)

    arrived_out(rec0, 0)
    for cb in range(COLB):
        cols = slice(cb * BLK, (cb + 1) * BLK)
        x1 = 2.0 * returned(rec0, cb) + tv[:, cols]
        nv[:, cols] = x1
        yw1[9 + cb] = x1.astype(jnp.bfloat16).reshape(TILES, TILE, BLK)
    ys1 = y_copies(yw1, 1)
    for c in ys1:
        c.start()
    stored = pltpu.make_async_copy(nv, next_hbm, store_sem.at[0])
    stored.start()
    for cb in range(COLB):
        cols = slice(cb * BLK, (cb + 1) * BLK)
        tv[:, cols] = 2.0 * (dv[:, cols] * nv[:, cols]) - xv[:, cols]
    for c in ys1:
        c.wait_recv()
    for cb in range(COLB):
        cols = slice(cb * BLK, (cb + 1) * BLK)
        tv[:, cols] = tv[:, cols] + 2.0 * beta(yw1, cb)
    arrived_out(rec1, 1)
    for cb in range(COLB):
        cols = slice(cb * BLK, (cb + 1) * BLK)
        ov[:, cols] = tv[:, cols] + 2.0 * returned(rec1, cb)
    last = pltpu.make_async_copy(ov, after_hbm, store_sem.at[1])
    last.start()

    for step in range(2):
        sent_in(step)

        @pl.when(is_home)
        def _(step=step):
            await_bytes(win0.at[pl.ds(0, (PIECES - 1) * TILES)], out_send.at[step])

    for c in ys0 + ys1:
        c.wait_send()
    stored.wait()
    last.wait()


def on_device(prev, this, diag, ablk, acls, aoff, amask, bblk, bcls, boff, bmask):
    rows, columns = ROWS, COLB * BLK
    f32, bf16 = jnp.float32, jnp.bfloat16
    hbm = pl.BlockSpec(memory_space=pltpu.HBM)
    smem = pl.BlockSpec(memory_space=pltpu.SMEM)
    dma = pltpu.SemaphoreType.DMA
    next_vector, after_vector = pl.pallas_call(
        kernel,
        out_shape=[jax.ShapeDtypeStruct((rows, columns), f32)] * 2,
        in_specs=[hbm, hbm, hbm, hbm, smem, smem, smem, hbm, smem, smem, smem],
        out_specs=[hbm, hbm],
        scratch_shapes=[
            *[pltpu.VMEM((rows, columns), f32)] * 6,
            *[pltpu.VMEM((YWIN, TILES, TILE, BLK), bf16)] * 2,
            pltpu.VMEM((COLB, TILES, TILE, BLK), bf16),
            *[pltpu.VMEM((PIECES * TILES, TILE, BLK), bf16)] * 5,
            *[pltpu.VMEM((4, COLB, TILES, TILE, BLK), bf16)] * 2,
            pltpu.VMEM((WIN, 2, BLK, BLK), bf16),
            pltpu.VMEM((COLB, 2, BLK, BLK), bf16),
            pltpu.VMEM((WIN, BLK, 2 * BLK), bf16),
            pltpu.VMEM((COLB, BLK, 2 * BLK), bf16),
            dma((8,)),
            dma((2,)),
            dma((2, 3)),
            dma((2,)),
            dma((2,)),
            dma((2, 2)),
            dma((2, 2, 4)),
            dma((4,)),
        ],
        compiler_params=pltpu.CompilerParams(
            collective_id=0, has_side_effects=True, vmem_limit_bytes=60 * 1024 * 1024
        ),
        name="chebyshev_steps",
    )(prev, this, diag, ablk, acls, aoff.T, amask.T, bblk, bcls, boff.T, bmask.T)
    return next_vector, after_vector


def solution(mesh):
    own = P("aa", "ba")
    return jax.shard_map(
        on_device,
        mesh=mesh,
        in_specs=(own, own, own, *[P()] * 8),
        out_specs=(own, own),
        check_vma=False,
    )
```

time: 181 us -> 45.8 us (0.25)
  the two profiles are of different devices: /device:TPU:8 before, /device:TPU:1 now
where the time goes in v1:
time: 45.8 us; the launch traced here: 45.6 us
  Pallas kernels  41.8 us (91%)
  local copies, waits for them, and re-layouts  3.16 us (7%)
  between operations  0.64 us (1%)
    pallas_call x1, Pallas kernels, on_device(): pl.pallas_call(kernel, out_shape=[jax.ShapeDtypeStruct((rows, columns), f...  41.8 us
    unnamed x2, local copies, waits for them, and re-layouts  3.16 us

profile of v1, /device:TPU:1, one launch (start us, length us, event | category | flops | bytes accessed | tf_op | source)
XLA Modules:
  0.0 45.6 jit_solution(4823250695639401439)
XLA Ops:
  0.6 41.8 %chebyshev_steps.1 = (f32[48,768]{1,0:T(8,128)}, f32[48,768]{1,0:T(8,128)}) custom-call(f32[48,768]{1,0:T(8,128)} %prev_hbm.1, f32[48,768]{1,0:T(8,128)} %this_hbm.1, f32[48,768]{1,0:T(8,128)} %diag_hbm.1, bf16[36,2,128,128]{3,2,1,0:T(8,128)(2,1)} %ablk_hbm.1, s32[8]{0:T(128)} %acls.1, s32[2,36]{1,0:T(2,128)} %bitcast.4, s32[2,36]{1,0:T(2,128)} %bitcast.5, ...), custom_call_target="tpu_custom_call" | custom-call | tf_op jit(solution)/shard_map/chebyshev_steps/pallas_call | solution.py:374
  42.4 1.6 %copy.15 = f32[48,768]{1,0:T(8,128)} copy(f32[48,768]{1,0:T(8,128)} %get-tuple-element.4) | data formatting | bytes 294912
  44.0 1.6 %copy.16 = f32[48,768]{1,0:T(8,128)} copy(f32[48,768]{1,0:T(8,128)} %get-tuple-element.5) | data formatting | bytes 294912

commit v2 on v1

--- a/solution.py
+++ b/solution.py
@@ -140,34 +140,28 @@
     def piece(k):
         return pl.ds(TILES * k, TILES)
 
-    def send_in(src, w, step):
+    def send_in(src, w, step, cb):
         @pl.when(reaches)
         def _():
-            for cb in range(COLB):
-                remote(
-                    src(cb), w.at[piece(3 * PLANE + p)],
-                    in_send.at[step, 0], in_recv.at[step], at(-2, cb),
-                ).start()
+            remote(
+                src, w.at[piece(3 * PLANE + p)],
+                in_send.at[step, 0], in_recv.at[step], at(-2, cb),
+            ).start()
 
         for d, base in ((-1, 2 * PLANE), (1, 0)):
-            for cb in range(COLB):
-                remote(
-                    src(cb), w.at[piece(base + p)], in_send.at[step, 1], in_recv.at[step], at(d, cb)
-                ).start()
-        for cb in range(COLB):
-
-            @pl.when(p != cb)
-            def _(cb=cb):
-                remote(
-                    src(cb), w.at[piece(PLANE + p)],
-                    in_send.at[step, 2], in_recv.at[step], at(0, cb),
-                ).start()
-
-            @pl.when(p == cb)
-            def _(cb=cb):
-                pltpu.make_async_copy(
-                    src(cb), w.at[piece(PLANE + p)], self_sem.at[step]
-                ).start()
+            remote(
+                src, w.at[piece(base + p)], in_send.at[step, 1], in_recv.at[step], at(d, cb)
+            ).start()
+
+        @pl.when(p != cb)
+        def _():
+            remote(
+                src, w.at[piece(PLANE + p)], in_send.at[step, 2], in_recv.at[step], at(0, cb)
+            ).start()
+
+        @pl.when(p == cb)
+        def _():
+            pltpu.make_async_copy(src, w.at[piece(PLANE + p)], self_sem.at[step]).start()
 
     def sent_in(step):
         @pl.when(reaches)
@@ -188,18 +182,21 @@
         await_bytes(w.at[pl.ds(0, (PIECES - 1) * TILES)], in_recv.at[step])
         await_bytes(w.at[pl.ds(0, TILES)], self_sem.at[step])
 
-    def send_out(src, rec, step):
+    def send_far(src, rec, step):
         for q in range(ROWB):
             remote(
                 src.at[piece(3 * PLANE + q)], rec.at[3, p],
                 out_send.at[step], out_recv.at[step, 1], at(2, q),
             ).start()
-        for d, base, slot in ((1, 2 * PLANE, 0), (-1, 0, 2)):
-            for q in range(PLANE):
-                remote(
-                    src.at[piece(base + q)], rec.at[slot, p],
-                    out_send.at[step], out_recv.at[step, 0], at(d, q),
-                ).start()
+
+    def send_near(src, rec, step, d, base, slot):
+        for q in range(PLANE):
+            remote(
+                src.at[piece(base + q)], rec.at[slot, p],
+                out_send.at[step], out_recv.at[step, 0], at(d, q),
+            ).start()
+
+    def send_own(src, rec, step):
         for k in range(1, PLANE):
             q = lax.rem(p + k, PLANE)
             remote(
@@ -227,7 +224,8 @@
     ys0 = y_copies(yw0, 0)
     for c in ys0:
         c.start()
-    send_in(lambda cb: yw0.at[9 + cb], win0, 0)
+    for cb in range(COLB):
+        send_in(yw0.at[9 + cb], win0, 0, cb)
 
     a_table = class_table(acls)
     b_table = class_table(bcls)
@@ -285,19 +283,28 @@
 
     def beta(w, r):
         both = jnp.concatenate([w[b_at[r][k]].reshape(ROWS, BLK) for k in range(2)], axis=1)
-        out = lax.dot_general(
+        return lax.dot_general(
             both, bw[r], (((1,), (1,)), ((), ())), preferred_element_type=jnp.float32
         )
-        return out.astype(jnp.bfloat16).astype(jnp.float32)
-
-    def alpha(w, out):
-        for j in range(WIN):
+
+    def alpha(w, out, rows):
+        for j in rows:
             both = jnp.concatenate(
                 [w[pl.ds(a_at[j][k] * 8, 8)].reshape(BLK, BLK) for k in range(2)], axis=0
             )
             product = jnp.dot(aw[j], both, preferred_element_type=jnp.float32)
             out[8 * j : 8 * (j + 1)] = product.astype(jnp.bfloat16).reshape(8, TILE, BLK)
 
+    def alpha_and_send(w, out, rec, step):
+        alpha(w, out, range(9, 10))
+        send_far(out, rec, step)
+        alpha(w, out, range(6, 9))
+        send_near(out, rec, step, 1, 2 * PLANE, 0)
+        alpha(w, out, range(0, 3))
+        send_near(out, rec, step, -1, 0, 2)
+        alpha(w, out, range(3, 6))
+        send_own(out, rec, step)
+
     def returned(rec, cb):
         return jnp.concatenate(
             [rec[slot_at[q], cb, q] for q in range(TILES)], axis=0
@@ -307,44 +314,39 @@
         c.wait_recv()
     for cb in range(COLB):
         cols = slice(cb * BLK, (cb + 1) * BLK)
-        t = 2.0 * (beta(yw0, cb) + dv[:, cols] * xv[:, cols]) - pv[:, cols]
+        b1 = beta(yw0, cb).astype(jnp.bfloat16).astype(jnp.float32)
+        t = 2.0 * (b1 + dv[:, cols] * xv[:, cols]) - pv[:, cols]
         tv[:, cols] = t
-        tb[cb] = t.astype(jnp.bfloat16).reshape(TILES, TILE, BLK)
-    send_in(lambda cb: tb.at[cb], wint, 1)
+        yw1[9 + cb] = t.astype(jnp.bfloat16).reshape(TILES, TILE, BLK)
+        tb[cb] = (t + 2.0 * b1).astype(jnp.bfloat16).reshape(TILES, TILE, BLK)
+        send_in(tb.at[cb], wint, 1, cb)
+    ys1 = y_copies(yw1, 1)
+    for c in ys1:
+        c.start()
 
     @pl.when(is_home)
     def _():
         arrived_in(win0, 0)
-        alpha(win0, al0)
-        send_out(al0, rec0, 0)
+        alpha_and_send(win0, al0, rec0, 0)
         arrived_in(wint, 1)
         for j in range(WIN):
             rows = slice(8 * j, 8 * (j + 1))
             win1[rows] = (
                 2.0 * al0[rows].astype(jnp.float32) + wint[rows].astype(jnp.float32)
             ).astype(jnp.bfloat16)
-        alpha(win1, al1)
-        send_out(al1, rec1, 1)
+        alpha_and_send(win1, al1, rec1, 1)
 
     arrived_out(rec0, 0)
     for cb in range(COLB):
         cols = slice(cb * BLK, (cb + 1) * BLK)
-        x1 = 2.0 * returned(rec0, cb) + tv[:, cols]
-        nv[:, cols] = x1
-        yw1[9 + cb] = x1.astype(jnp.bfloat16).reshape(TILES, TILE, BLK)
-    ys1 = y_copies(yw1, 1)
-    for c in ys1:
-        c.start()
+        nv[:, cols] = 2.0 * returned(rec0, cb) + tv[:, cols]
     stored = pltpu.make_async_copy(nv, next_hbm, store_sem.at[0])
     stored.start()
-    for cb in range(COLB):
-        cols = slice(cb * BLK, (cb + 1) * BLK)
-        tv[:, cols] = 2.0 * (dv[:, cols] * nv[:, cols]) - xv[:, cols]
     for c in ys1:
         c.wait_recv()
     for cb in range(COLB):
         cols = slice(cb * BLK, (cb + 1) * BLK)
-        tv[:, cols] = tv[:, cols] + 2.0 * beta(yw1, cb)
+        tv[:, cols] = 2.0 * (beta(yw1, cb) + dv[:, cols] * nv[:, cols]) - xv[:, cols]
     arrived_out(rec1, 1)
     for cb in range(COLB):
         cols = slice(cb * BLK, (cb + 1) * BLK)
@@ -363,6 +365,19 @@
         c.wait_send()
     stored.wait()
     last.wait()
+
+
+def hand_over(next_in, after_in, next_out, after_out, held, sem):
+    pairs = ((next_in, next_out), (after_in, after_out))
+    taken = [pltpu.make_async_copy(c[0], held.at[k], sem.at[0, k]) for k, c in enumerate(pairs)]
+    given = [pltpu.make_async_copy(held.at[k], c[1], sem.at[1, k]) for k, c in enumerate(pairs)]
+    for c in taken:
+        c.start()
+    for k in range(2):
+        taken[k].wait()
+        given[k].start()
+    for c in given:
+        c.wait()
 
 
 def on_device(prev, this, diag, ablk, acls, aoff, amask, bblk, bcls, boff, bmask):
@@ -400,7 +415,15 @@
         ),
         name="chebyshev_steps",
     )(prev, this, diag, ablk, acls, aoff.T, amask.T, bblk, bcls, boff.T, bmask.T)
-    return next_vector, after_vector
+    return pl.pallas_call(
+        hand_over,
+        out_shape=[jax.ShapeDtypeStruct((rows, columns), f32)] * 2,
+        in_specs=[hbm, hbm],
+        out_specs=[hbm, hbm],
+        scratch_shapes=[pltpu.VMEM((2, rows, columns), f32), dma((2, 2))],
+        compiler_params=pltpu.CompilerParams(vmem_limit_bytes=60 * 1024 * 1024),
+        name="hand_over",
+    )(next_vector, after_vector)
 
 
 def solution(mesh):

time: 45.8 us -> 44.4 us (0.969)
  local copies, waits for them, and re-layouts: 3.16 us -> 0 us
  Pallas kernels: 41.8 us -> 43.6 us
    unnamed x2 -> x0, local copies, waits for them, and re-layouts: 3.16 us -> none
    pallas_call x0 -> x1, Pallas kernels: none -> 1.68 us  [on_device(): pl.pallas_call(hand_over, out_shape=[jax.ShapeDtypeStruct((rows, columns)...]
where the time goes in v2:
time: 44.4 us; the launch traced here: 44.2 us
  Pallas kernels  43.6 us (98%)
  between operations  0.64 us (1%)
    pallas_call x1, Pallas kernels, on_device(): pl.pallas_call(kernel, out_shape=[jax.ShapeDtypeStruct((rows, columns), f...  41.9 us
    pallas_call x1, Pallas kernels, on_device(): pl.pallas_call(hand_over, out_shape=[jax.ShapeDtypeStruct((rows, columns)...  1.68 us

profile of v2, /device:TPU:1, one launch (start us, length us, event | category | flops | bytes accessed | tf_op | source)
XLA Modules:
  0.0 44.2 jit_solution(6895872957532222734)
XLA Ops:
  0.6 41.9 %chebyshev_steps.1 = (f32[48,768]{1,0:T(8,128)}, f32[48,768]{1,0:T(8,128)}) custom-call(f32[48,768]{1,0:T(8,128)} %prev_hbm.1, f32[48,768]{1,0:T(8,128)} %this_hbm.1, f32[48,768]{1,0:T(8,128)} %diag_hbm.1, bf16[36,2,128,128]{3,2,1,0:T(8,128)(2,1)} %ablk_hbm.1, s32[8]{0:T(128)} %acls.1, s32[2,36]{1,0:T(2,128)} %bitcast.4, s32[2,36]{1,0:T(2,128)} %bitcast.5, ...), custom_call_target="tpu_custom_call" | custom-call | tf_op jit(solution)/shard_map/chebyshev_steps/pallas_call | solution.py:389
  42.6 1.7 %hand_over.1 = (f32[48,768]{1,0:T(8,128)}, f32[48,768]{1,0:T(8,128)}) custom-call(f32[48,768]{1,0:T(8,128)} %get-tuple-element.4.next_in, f32[48,768]{1,0:T(8,128)} %get-tuple-element.5.after_in), custom_call_target="tpu_custom_call" | custom-call | tf_op jit(solution)/shard_map/hand_over/pallas_call | solution.py:418

commit v3 on v2

--- a/solution.py
+++ b/solution.py
@@ -11,6 +11,7 @@
 LINE = 8
 ROWS = 48
 COLB = 6
+HOME = 2
 ROWB = 3
 WIN = 10
 TILE = 16
@@ -67,17 +68,18 @@
     y = lax.axis_index("ba")
     z = lax.div(aa, PLANE)
     p = lax.rem(aa, PLANE)
-    plane = {d: lax.rem(z + d + PLANES, PLANES) for d in (-2, -1, 0, 1, 2)}
-    first = {d: plane[d] * PLANE for d in plane}
-    line = {d: lax.rem(y + d + LINE, LINE) for d in (-2, -1, 1, 2)}
-    is_home = p < COLB
+    is_home = p >= HOME
     reaches = p < ROWB
+    has_plane = {d: (z >= -d) if d < 0 else (z < PLANES - d) for d in (-2, -1, 1, 2)}
+    has_line = {d: (y >= -d) if d < 0 else (y < LINE - d) for d in (-2, -1, 1, 2)}
+    sends_far = jnp.logical_and(reaches, has_plane[-2])
+    homes_far = jnp.logical_and(is_home, has_plane[2])
 
     def at(d, q):
-        return {"aa": first[d] + q, "ba": y}
+        return {"aa": aa + (d * PLANE - p) + q, "ba": y}
 
     def along(d):
-        return {"aa": aa, "ba": line[d]}
+        return {"aa": aa, "ba": y + d}
 
     loads = [pltpu.make_async_copy(this_hbm, xv, load_sem.at[0])]
     loads[0].start()
@@ -88,19 +90,27 @@
         pl.semaphore_signal(barrier, inc=1, device_id=to, device_id_type=MESH)
 
     for d in (-2, -1, 1, 2):
-        greet(along(d))
+
+        @pl.when(has_line[d])
+        def _(d=d):
+            greet(along(d))
+
     for d in (-1, 1):
-        for q in range(PLANE):
-            greet(at(d, q))
+
+        @pl.when(has_plane[d])
+        def _(d=d):
+            for q in range(PLANE):
+                greet(at(d, q))
+
     for q in range(1, PLANE):
         greet(at(0, lax.rem(p + q, PLANE)))
 
-    @pl.when(reaches)
+    @pl.when(sends_far)
     def _():
-        for q in range(COLB):
-            greet(at(-2, q))
-
-    @pl.when(is_home)
+        for cb in range(COLB):
+            greet(at(-2, HOME + cb))
+
+    @pl.when(homes_far)
     def _():
         for q in range(ROWB):
             greet(at(2, q))
@@ -111,9 +121,10 @@
         pltpu.make_async_copy(bblk_hbm.at[pl.ds(y * COLB, COLB)], braw, load_sem.at[3]),
     ]
     for k, (d, count) in enumerate(((-1, ROWB), (0, ROWB), (1, ROWB), (2, 1))):
+        held = lax.rem(z + d + PLANES, PLANES)
         loads.append(
             pltpu.make_async_copy(
-                ablk_hbm.at[pl.ds(plane[d] * ROWB, count)],
+                ablk_hbm.at[pl.ds(held * ROWB, count)],
                 araw.at[pl.ds(ROWB * k, count)],
                 load_sem.at[4 + k],
             )
@@ -125,105 +136,122 @@
     for cb in range(COLB):
         yw0[9 + cb] = xv[:, cb * BLK : (cb + 1) * BLK].astype(jnp.bfloat16).reshape(TILES, TILE, BLK)
 
-    pl.semaphore_wait(barrier, 27 + jnp.where(reaches, COLB, 0) + jnp.where(is_home, ROWB, 0))
-
-    def y_copies(w, step):
-        parts = ((9, 6, 3, 1), (9, 6, 15, -1), (12, 3, 0, 2), (9, 3, 21, -2))
-        return [
-            remote(
-                w.at[pl.ds(src, n)], w.at[pl.ds(dst, n)],
-                y_sem.at[step, 0, k], y_sem.at[step, 1, k], along(d),
-            )
-            for k, (src, n, dst, d) in enumerate(parts)
-        ]
+    greetings = PLANE - 1 + jnp.where(sends_far, COLB, 0) + jnp.where(homes_far, ROWB, 0)
+    for d in (-2, -1, 1, 2):
+        greetings = greetings + jnp.where(has_line[d], 1, 0)
+    for d in (-1, 1):
+        greetings = greetings + jnp.where(has_plane[d], PLANE, 0)
+    pl.semaphore_wait(barrier, greetings)
+
+    def y_copy(w, step, k):
+        src, n, dst, d = ((9, 6, 3, 1), (9, 6, 15, -1), (12, 3, 0, 2), (9, 3, 21, -2))[k]
+        return d, remote(
+            w.at[pl.ds(src, n)], w.at[pl.ds(dst, n)],
+            y_sem.at[step, 0, k], y_sem.at[step, 1, k], along(d),
+        )
+
+    def y_start(w, step):
+        for k in range(4):
+            d, copy = y_copy(w, step, k)
+            pl.when(has_line[d])(copy.start)
+
+    def y_sent(w, step):
+        for k in range(4):
+            d, copy = y_copy(w, step, k)
+            pl.when(has_line[d])(copy.wait_send)
+
+    def y_arrived(w, step):
+        for k in range(4):
+            d, copy = y_copy(w, step, k)
+            pl.when(has_line[-d])(copy.wait_recv)
 
     def piece(k):
         return pl.ds(TILES * k, TILES)
 
     def send_in(src, w, step, cb):
-        @pl.when(reaches)
+        to = HOME + cb
+
+        @pl.when(sends_far)
         def _():
             remote(
                 src, w.at[piece(3 * PLANE + p)],
-                in_send.at[step, 0], in_recv.at[step], at(-2, cb),
+                in_send.at[step, 3], in_recv.at[step, 3], at(-2, to),
             ).start()
 
-        for d, base in ((-1, 2 * PLANE), (1, 0)):
-            remote(
-                src, w.at[piece(base + p)], in_send.at[step, 1], in_recv.at[step], at(d, cb)
-            ).start()
-
-        @pl.when(p != cb)
+        for k, d, base in ((2, -1, 2 * PLANE), (0, 1, 0)):
+
+            @pl.when(has_plane[d])
+            def _(k=k, d=d, base=base):
+                remote(
+                    src, w.at[piece(base + p)],
+                    in_send.at[step, k], in_recv.at[step, k], at(d, to),
+                ).start()
+
+        @pl.when(p != to)
         def _():
             remote(
-                src, w.at[piece(PLANE + p)], in_send.at[step, 2], in_recv.at[step], at(0, cb)
+                src, w.at[piece(PLANE + p)], in_send.at[step, 1], in_recv.at[step, 1], at(0, to)
             ).start()
 
-        @pl.when(p == cb)
+        @pl.when(p == to)
         def _():
             pltpu.make_async_copy(src, w.at[piece(PLANE + p)], self_sem.at[step]).start()
 
+    def await_pieces(count, sem):
+        await_bytes(win0.at[pl.ds(0, count * TILES)], sem)
+
     def sent_in(step):
-        @pl.when(reaches)
+        pl.when(sends_far)(lambda: await_pieces(COLB, in_send.at[step, 3]))
+        pl.when(has_plane[-1])(lambda: await_pieces(COLB, in_send.at[step, 2]))
+        pl.when(has_plane[1])(lambda: await_pieces(COLB, in_send.at[step, 0]))
+        pl.when(is_home)(lambda: await_pieces(COLB - 1, in_send.at[step, 1]))
+        pl.when(jnp.logical_not(is_home))(lambda: await_pieces(COLB, in_send.at[step, 1]))
+
+    def arrived_in(step):
+        await_pieces(1, self_sem.at[step])
+        await_pieces(PLANE - 1, in_recv.at[step, 1])
+        pl.when(has_plane[-1])(lambda: await_pieces(PLANE, in_recv.at[step, 0]))
+        pl.when(has_plane[1])(lambda: await_pieces(PLANE, in_recv.at[step, 2]))
+        pl.when(has_plane[2])(lambda: await_pieces(ROWB, in_recv.at[step, 3]))
+
+    def send_out(src, rec, step, d, base, slot, count):
+        @pl.when(has_plane[d])
         def _():
-            await_bytes(win0.at[pl.ds(0, COLB * TILES)], in_send.at[step, 0])
-
-        await_bytes(win0.at[pl.ds(0, 2 * COLB * TILES)], in_send.at[step, 1])
-
-        @pl.when(is_home)
-        def _():
-            await_bytes(win0.at[pl.ds(0, (COLB - 1) * TILES)], in_send.at[step, 2])
-
-        @pl.when(jnp.logical_not(is_home))
-        def _():
-            await_bytes(win0.at[pl.ds(0, COLB * TILES)], in_send.at[step, 2])
-
-    def arrived_in(w, step):
-        await_bytes(w.at[pl.ds(0, (PIECES - 1) * TILES)], in_recv.at[step])
-        await_bytes(w.at[pl.ds(0, TILES)], self_sem.at[step])
-
-    def send_far(src, rec, step):
-        for q in range(ROWB):
-            remote(
-                src.at[piece(3 * PLANE + q)], rec.at[3, p],
-                out_send.at[step], out_recv.at[step, 1], at(2, q),
-            ).start()
-
-    def send_near(src, rec, step, d, base, slot):
-        for q in range(PLANE):
-            remote(
-                src.at[piece(base + q)], rec.at[slot, p],
-                out_send.at[step], out_recv.at[step, 0], at(d, q),
-            ).start()
+            for q in range(count):
+                remote(
+                    src.at[piece(base + q)], rec.at[slot, p - HOME],
+                    out_send.at[step, slot], out_recv.at[step, slot], at(d, q),
+                ).start()
 
     def send_own(src, rec, step):
         for k in range(1, PLANE):
             q = lax.rem(p + k, PLANE)
             remote(
-                src.at[piece(PLANE + q)], rec.at[1, p],
-                out_send.at[step], out_recv.at[step, 0], at(0, q),
+                src.at[piece(PLANE + q)], rec.at[1, p - HOME],
+                out_send.at[step, 1], out_recv.at[step, 1], at(0, q),
             ).start()
         pltpu.make_async_copy(
-            src.at[piece(PLANE + p)], rec.at[1, p], self_sem.at[2 + step]
+            src.at[piece(PLANE + p)], rec.at[1, p - HOME], self_sem.at[2 + step]
         ).start()
 
-    def arrived_out(rec, step):
-        @pl.when(reaches)
-        def _():
-            await_bytes(rec.at[3], out_recv.at[step, 1])
+    def sent_out(step):
+        await_pieces(PLANE - 1, out_send.at[step, 1])
+        pl.when(has_plane[2])(lambda: await_pieces(ROWB, out_send.at[step, 3]))
+        pl.when(has_plane[1])(lambda: await_pieces(PLANE, out_send.at[step, 0]))
+        pl.when(has_plane[-1])(lambda: await_pieces(PLANE, out_send.at[step, 2]))
+
+    def arrived_out(step):
+        pl.when(sends_far)(lambda: await_pieces(COLB, out_recv.at[step, 3]))
+        pl.when(has_plane[-1])(lambda: await_pieces(COLB, out_recv.at[step, 0]))
+        pl.when(has_plane[1])(lambda: await_pieces(COLB, out_recv.at[step, 2]))
+        pl.when(jnp.logical_not(is_home))(lambda: await_pieces(COLB, out_recv.at[step, 1]))
 
         @pl.when(is_home)
         def _():
-            await_bytes(win0.at[pl.ds(0, (3 * COLB - 1) * TILES)], out_recv.at[step, 0])
-            await_bytes(rec.at[3, 0], self_sem.at[2 + step])
-
-        @pl.when(jnp.logical_not(is_home))
-        def _():
-            await_bytes(win0.at[pl.ds(0, 3 * COLB * TILES)], out_recv.at[step, 0])
-
-    ys0 = y_copies(yw0, 0)
-    for c in ys0:
-        c.start()
+            await_pieces(COLB - 1, out_recv.at[step, 1])
+            await_pieces(1, self_sem.at[2 + step])
+
+    y_start(yw0, 0)
     for cb in range(COLB):
         send_in(yw0.at[9 + cb], win0, 0, cb)
 
@@ -297,11 +325,11 @@
 
     def alpha_and_send(w, out, rec, step):
         alpha(w, out, range(9, 10))
-        send_far(out, rec, step)
+        send_out(out, rec, step, 2, 3 * PLANE, 3, ROWB)
         alpha(w, out, range(6, 9))
-        send_near(out, rec, step, 1, 2 * PLANE, 0)
+        send_out(out, rec, step, 1, 2 * PLANE, 0, PLANE)
         alpha(w, out, range(0, 3))
-        send_near(out, rec, step, -1, 0, 2)
+        send_out(out, rec, step, -1, 0, 2, PLANE)
         alpha(w, out, range(3, 6))
         send_own(out, rec, step)
 
@@ -310,8 +338,7 @@
             [rec[slot_at[q], cb, q] for q in range(TILES)], axis=0
         ).astype(jnp.float32)
 
-    for c in ys0:
-        c.wait_recv()
+    y_arrived(yw0, 0)
     for cb in range(COLB):
         cols = slice(cb * BLK, (cb + 1) * BLK)
         b1 = beta(yw0, cb).astype(jnp.bfloat16).astype(jnp.float32)
@@ -320,15 +347,13 @@
         yw1[9 + cb] = t.astype(jnp.bfloat16).reshape(TILES, TILE, BLK)
         tb[cb] = (t + 2.0 * b1).astype(jnp.bfloat16).reshape(TILES, TILE, BLK)
         send_in(tb.at[cb], wint, 1, cb)
-    ys1 = y_copies(yw1, 1)
-    for c in ys1:
-        c.start()
+    y_start(yw1, 1)
 
     @pl.when(is_home)
     def _():
-        arrived_in(win0, 0)
+        arrived_in(0)
         alpha_and_send(win0, al0, rec0, 0)
-        arrived_in(wint, 1)
+        arrived_in(1)
         for j in range(WIN):
             rows = slice(8 * j, 8 * (j + 1))
             win1[rows] = (
@@ -336,18 +361,17 @@
             ).astype(jnp.bfloat16)
         alpha_and_send(win1, al1, rec1, 1)
 
-    arrived_out(rec0, 0)
+    arrived_out(0)
     for cb in range(COLB):
         cols = slice(cb * BLK, (cb + 1) * BLK)
         nv[:, cols] = 2.0 * returned(rec0, cb) + tv[:, cols]
     stored = pltpu.make_async_copy(nv, next_hbm, store_sem.at[0])
     stored.start()
-    for c in ys1:
-        c.wait_recv()
+    y_arrived(yw1, 1)
     for cb in range(COLB):
         cols = slice(cb * BLK, (cb + 1) * BLK)
         tv[:, cols] = 2.0 * (beta(yw1, cb) + dv[:, cols] * nv[:, cols]) - xv[:, cols]
-    arrived_out(rec1, 1)
+    arrived_out(1)
     for cb in range(COLB):
         cols = slice(cb * BLK, (cb + 1) * BLK)
         ov[:, cols] = tv[:, cols] + 2.0 * returned(rec1, cb)
@@ -356,13 +380,9 @@
 
     for step in range(2):
         sent_in(step)
-
-        @pl.when(is_home)
-        def _(step=step):
-            await_bytes(win0.at[pl.ds(0, (PIECES - 1) * TILES)], out_send.at[step])
-
-    for c in ys0 + ys1:
-        c.wait_send()
+        pl.when(is_home)(lambda step=step: sent_out(step))
+    y_sent(yw0, 0)
+    y_sent(yw1, 1)
     stored.wait()
     last.wait()
 
@@ -403,10 +423,7 @@
             pltpu.VMEM((COLB, BLK, 2 * BLK), bf16),
             dma((8,)),
             dma((2,)),
-            dma((2, 3)),
-            dma((2,)),
-            dma((2,)),
-            dma((2, 2)),
+            *[dma((2, 4))] * 4,
             dma((2, 2, 4)),
             dma((4,)),
         ],

time: 44.4 us -> 35.4 us (0.80)
  the two profiles are of different devices: /device:TPU:1 before, /device:TPU:81 now
where the time goes in v3:
time: 35.4 us; the launch traced here: 35.2 us
  Pallas kernels  34.5 us (97%)
  between operations  0.64 us (2%)
    pallas_call x1, Pallas kernels, on_device(): pl.pallas_call(kernel, out_shape=[jax.ShapeDtypeStruct((rows, columns), f...  32.9 us
    pallas_call x1, Pallas kernels, on_device(): pl.pallas_call(hand_over, out_shape=[jax.ShapeDtypeStruct((rows, columns)...  1.68 us

profile of v3, /device:TPU:81, one launch (start us, length us, event | category | flops | bytes accessed | tf_op | source)
XLA Modules:
  0.0 35.2 jit_solution(7270763015694250634)
XLA Ops:
  0.6 32.9 %chebyshev_steps.1 = (f32[48,768]{1,0:T(8,128)}, f32[48,768]{1,0:T(8,128)}) custom-call(f32[48,768]{1,0:T(8,128)} %prev_hbm.1, f32[48,768]{1,0:T(8,128)} %this_hbm.1, f32[48,768]{1,0:T(8,128)} %diag_hbm.1, bf16[36,2,128,128]{3,2,1,0:T(8,128)(2,1)} %ablk_hbm.1, s32[8]{0:T(128)} %acls.1, s32[2,36]{1,0:T(2,128)} %bitcast.4, s32[2,36]{1,0:T(2,128)} %bitcast.5, ...), custom_call_target="tpu_custom_call" | custom-call | tf_op jit(solution)/shard_map/chebyshev_steps/pallas_call | solution.py:409
  33.5 1.7 %hand_over.1 = (f32[48,768]{1,0:T(8,128)}, f32[48,768]{1,0:T(8,128)}) custom-call(f32[48,768]{1,0:T(8,128)} %get-tuple-element.4.next_in, f32[48,768]{1,0:T(8,128)} %get-tuple-element.5.after_in), custom_call_target="tpu_custom_call" | custom-call | tf_op jit(solution)/shard_map/hand_over/pallas_call | solution.py:435

commit v4 on v3

--- a/solution.py
+++ b/solution.py
@@ -16,6 +16,7 @@
 WIN = 10
 TILE = 16
 TILES = 3
+PARTS = ((0, 1), (1, 1), (2, 1))
 PIECES = 27
 YWIN = 24
 NCLS = 8
@@ -60,10 +61,11 @@
 
 def kernel(
     prev_hbm, this_hbm, diag_hbm, ablk_hbm, acls, aoff, amask, bblk_hbm, bcls, boff, bmask,
-    next_hbm, after_hbm,
-    xv, pv, dv, tv, nv, ov, yw0, yw1, tb, win0, wint, win1, al0, al1, rec0, rec1, araw, braw, aw, bw,
-    load_sem, store_sem, in_send, in_recv, out_send, out_recv, y_sem, self_sem,
+    nv, ov,
+    xv, pv, dv, tv, xb, yw1, pre, win0, wint, al0, al1, rec0, rec1, araw, braw, aw, bw,
+    load_sem, in_send, in_recv, out_send, out_recv, y_sem, self_sem, *parts,
 ):
+    yw0, tb = parts[: len(PARTS)], parts[len(PARTS) :]
     aa = lax.axis_index("aa")
     y = lax.axis_index("ba")
     z = lax.div(aa, PLANE)
@@ -134,7 +136,10 @@
 
     loads[0].wait()
     for cb in range(COLB):
-        yw0[9 + cb] = xv[:, cb * BLK : (cb + 1) * BLK].astype(jnp.bfloat16).reshape(TILES, TILE, BLK)
+        own = xv[:, cb * BLK : (cb + 1) * BLK].astype(jnp.bfloat16).reshape(TILES, TILE, BLK)
+        xb[cb] = own
+        for k, (tile, tiles) in enumerate(PARTS):
+            yw0[k][9 + cb] = own[tile : tile + tiles]
 
     greetings = PLANE - 1 + jnp.where(sends_far, COLB, 0) + jnp.where(homes_far, ROWB, 0)
     for d in (-2, -1, 1, 2):
@@ -143,38 +148,41 @@
         greetings = greetings + jnp.where(has_plane[d], PLANE, 0)
     pl.semaphore_wait(barrier, greetings)
 
-    def y_copy(w, step, k):
+    def y_copy(w, at_sem, k):
         src, n, dst, d = ((9, 6, 3, 1), (9, 6, 15, -1), (12, 3, 0, 2), (9, 3, 21, -2))[k]
         return d, remote(
             w.at[pl.ds(src, n)], w.at[pl.ds(dst, n)],
-            y_sem.at[step, 0, k], y_sem.at[step, 1, k], along(d),
-        )
-
-    def y_start(w, step):
+            y_sem.at[at_sem, 0, k], y_sem.at[at_sem, 1, k], along(d),
+        )
+
+    def y_start(w, at_sem):
         for k in range(4):
-            d, copy = y_copy(w, step, k)
+            d, copy = y_copy(w, at_sem, k)
             pl.when(has_line[d])(copy.start)
 
-    def y_sent(w, step):
+    def y_sent(w, at_sem):
         for k in range(4):
-            d, copy = y_copy(w, step, k)
+            d, copy = y_copy(w, at_sem, k)
             pl.when(has_line[d])(copy.wait_send)
 
-    def y_arrived(w, step):
+    def y_arrived(w, at_sem):
         for k in range(4):
-            d, copy = y_copy(w, step, k)
+            d, copy = y_copy(w, at_sem, k)
             pl.when(has_line[-d])(copy.wait_recv)
 
     def piece(k):
         return pl.ds(TILES * k, TILES)
 
-    def send_in(src, w, step, cb):
+    def send_in(src, w, step, cb, tile, tiles):
         to = HOME + cb
+
+        def place(k):
+            return w.at[pl.ds(TILES * k + tile, tiles)]
 
         @pl.when(sends_far)
         def _():
             remote(
-                src, w.at[piece(3 * PLANE + p)],
+                src, place(3 * PLANE + p),
                 in_send.at[step, 3], in_recv.at[step, 3], at(-2, to),
             ).start()
 
@@ -183,19 +191,19 @@
             @pl.when(has_plane[d])
             def _(k=k, d=d, base=base):
                 remote(
-                    src, w.at[piece(base + p)],
+                    src, place(base + p),
                     in_send.at[step, k], in_recv.at[step, k], at(d, to),
                 ).start()
 
         @pl.when(p != to)
         def _():
             remote(
-                src, w.at[piece(PLANE + p)], in_send.at[step, 1], in_recv.at[step, 1], at(0, to)
+                src, place(PLANE + p), in_send.at[step, 1], in_recv.at[step, 1], at(0, to)
             ).start()
 
         @pl.when(p == to)
         def _():
-            pltpu.make_async_copy(src, w.at[piece(PLANE + p)], self_sem.at[step]).start()
+            pltpu.make_async_copy(src, place(PLANE + p), self_sem.at[step]).start()
 
     def await_pieces(count, sem):
         await_bytes(win0.at[pl.ds(0, count * TILES)], sem)
@@ -251,9 +259,10 @@
             await_pieces(COLB - 1, out_recv.at[step, 1])
             await_pieces(1, self_sem.at[2 + step])
 
-    y_start(yw0, 0)
+    for k in range(len(PARTS)):
+        y_start(yw0[k], k)
     for cb in range(COLB):
-        send_in(yw0.at[9 + cb], win0, 0, cb)
+        send_in(xb.at[cb], win0, 0, cb, 0, TILES)
 
     a_table = class_table(acls)
     b_table = class_table(bcls)
@@ -309,28 +318,33 @@
         al0[8 * WIN] = jnp.zeros((TILE, BLK), jnp.bfloat16)
         al1[8 * WIN] = jnp.zeros((TILE, BLK), jnp.bfloat16)
 
-    def beta(w, r):
-        both = jnp.concatenate([w[b_at[r][k]].reshape(ROWS, BLK) for k in range(2)], axis=1)
+    def beta(w, r, rows):
+        both = jnp.concatenate([w[b_at[r][k]].reshape(rows, BLK) for k in range(2)], axis=1)
         return lax.dot_general(
             both, bw[r], (((1,), (1,)), ((), ())), preferred_element_type=jnp.float32
         )
 
-    def alpha(w, out, rows):
+    def couple(w, j):
+        both = jnp.concatenate(
+            [w[pl.ds(a_at[j][k] * 8, 8)].reshape(BLK, BLK) for k in range(2)], axis=0
+        )
+        return jnp.dot(aw[j], both, preferred_element_type=jnp.float32)
+
+    def alpha(w, out, rows, more):
         for j in rows:
-            both = jnp.concatenate(
-                [w[pl.ds(a_at[j][k] * 8, 8)].reshape(BLK, BLK) for k in range(2)], axis=0
-            )
-            product = jnp.dot(aw[j], both, preferred_element_type=jnp.float32)
+            product = couple(w, j)
+            if more:
+                product = product + pre[j]
             out[8 * j : 8 * (j + 1)] = product.astype(jnp.bfloat16).reshape(8, TILE, BLK)
 
-    def alpha_and_send(w, out, rec, step):
-        alpha(w, out, range(9, 10))
+    def alpha_and_send(w, out, rec, step, more):
+        alpha(w, out, range(9, 10), more)
         send_out(out, rec, step, 2, 3 * PLANE, 3, ROWB)
-        alpha(w, out, range(6, 9))
+        alpha(w, out, range(6, 9), more)
         send_out(out, rec, step, 1, 2 * PLANE, 0, PLANE)
-        alpha(w, out, range(0, 3))
+        alpha(w, out, range(0, 3), more)
         send_out(out, rec, step, -1, 0, 2, PLANE)
-        alpha(w, out, range(3, 6))
+        alpha(w, out, range(3, 6), more)
         send_own(out, rec, step)
 
     def returned(rec, cb):
@@ -338,65 +352,57 @@
             [rec[slot_at[q], cb, q] for q in range(TILES)], axis=0
         ).astype(jnp.float32)
 
-    y_arrived(yw0, 0)
-    for cb in range(COLB):
-        cols = slice(cb * BLK, (cb + 1) * BLK)
-        b1 = beta(yw0, cb).astype(jnp.bfloat16).astype(jnp.float32)
-        t = 2.0 * (b1 + dv[:, cols] * xv[:, cols]) - pv[:, cols]
-        tv[:, cols] = t
-        yw1[9 + cb] = t.astype(jnp.bfloat16).reshape(TILES, TILE, BLK)
-        tb[cb] = (t + 2.0 * b1).astype(jnp.bfloat16).reshape(TILES, TILE, BLK)
-        send_in(tb.at[cb], wint, 1, cb)
-    y_start(yw1, 1)
+    for k, (tile, tiles) in enumerate(PARTS):
+        rows = slice(TILE * tile, TILE * (tile + tiles))
+        y_arrived(yw0[k], k)
+        for cb in range(COLB):
+            cols = slice(cb * BLK, (cb + 1) * BLK)
+            b1 = beta(yw0[k], cb, TILE * tiles).astype(jnp.bfloat16).astype(jnp.float32)
+            t = 2.0 * (b1 + dv[rows, cols] * xv[rows, cols]) - pv[rows, cols]
+            tv[rows, cols] = t
+            yw1[9 + cb, tile : tile + tiles] = t.astype(jnp.bfloat16).reshape(tiles, TILE, BLK)
+            tb[k][cb] = (t + 2.0 * b1).astype(jnp.bfloat16).reshape(tiles, TILE, BLK)
+            send_in(tb[k].at[cb], wint, 1, cb, tile, tiles)
+    y_start(yw1, len(PARTS))
 
     @pl.when(is_home)
     def _():
         arrived_in(0)
-        alpha_and_send(win0, al0, rec0, 0)
+        alpha_and_send(win0, al0, rec0, 0, False)
+        for j in range(WIN):
+            pre[j] = 2.0 * couple(al0, j)
         arrived_in(1)
-        for j in range(WIN):
-            rows = slice(8 * j, 8 * (j + 1))
-            win1[rows] = (
-                2.0 * al0[rows].astype(jnp.float32) + wint[rows].astype(jnp.float32)
-            ).astype(jnp.bfloat16)
-        alpha_and_send(win1, al1, rec1, 1)
+        alpha_and_send(wint, al1, rec1, 1, True)
 
     arrived_out(0)
     for cb in range(COLB):
         cols = slice(cb * BLK, (cb + 1) * BLK)
         nv[:, cols] = 2.0 * returned(rec0, cb) + tv[:, cols]
-    stored = pltpu.make_async_copy(nv, next_hbm, store_sem.at[0])
-    stored.start()
-    y_arrived(yw1, 1)
+    y_arrived(yw1, len(PARTS))
     for cb in range(COLB):
         cols = slice(cb * BLK, (cb + 1) * BLK)
-        tv[:, cols] = 2.0 * (beta(yw1, cb) + dv[:, cols] * nv[:, cols]) - xv[:, cols]
+        tv[:, cols] = 2.0 * (beta(yw1, cb, ROWS) + dv[:, cols] * nv[:, cols]) - xv[:, cols]
     arrived_out(1)
     for cb in range(COLB):
         cols = slice(cb * BLK, (cb + 1) * BLK)
         ov[:, cols] = tv[:, cols] + 2.0 * returned(rec1, cb)
-    last = pltpu.make_async_copy(ov, after_hbm, store_sem.at[1])
-    last.start()
 
     for step in range(2):
         sent_in(step)
         pl.when(is_home)(lambda step=step: sent_out(step))
-    y_sent(yw0, 0)
-    y_sent(yw1, 1)
-    stored.wait()
-    last.wait()
-
-
-def hand_over(next_in, after_in, next_out, after_out, held, sem):
-    pairs = ((next_in, next_out), (after_in, after_out))
-    taken = [pltpu.make_async_copy(c[0], held.at[k], sem.at[0, k]) for k, c in enumerate(pairs)]
-    given = [pltpu.make_async_copy(held.at[k], c[1], sem.at[1, k]) for k, c in enumerate(pairs)]
-    for c in taken:
+    for k in range(len(PARTS)):
+        y_sent(yw0[k], k)
+    y_sent(yw1, len(PARTS))
+
+
+def hand_over(next_in, after_in, next_out, after_out, sem):
+    copies = [
+        pltpu.make_async_copy(next_in, next_out, sem.at[0]),
+        pltpu.make_async_copy(after_in, after_out, sem.at[1]),
+    ]
+    for c in copies:
         c.start()
-    for k in range(2):
-        taken[k].wait()
-        given[k].start()
-    for c in given:
+    for c in copies:
         c.wait()
 
 
@@ -404,28 +410,31 @@
     rows, columns = ROWS, COLB * BLK
     f32, bf16 = jnp.float32, jnp.bfloat16
     hbm = pl.BlockSpec(memory_space=pltpu.HBM)
+    vmem = pl.BlockSpec(memory_space=pltpu.VMEM)
     smem = pl.BlockSpec(memory_space=pltpu.SMEM)
     dma = pltpu.SemaphoreType.DMA
     next_vector, after_vector = pl.pallas_call(
         kernel,
-        out_shape=[jax.ShapeDtypeStruct((rows, columns), f32)] * 2,
+        out_shape=[pltpu.VMEM((rows, columns), f32)] * 2,
         in_specs=[hbm, hbm, hbm, hbm, smem, smem, smem, hbm, smem, smem, smem],
-        out_specs=[hbm, hbm],
+        out_specs=[vmem, vmem],
         scratch_shapes=[
-            *[pltpu.VMEM((rows, columns), f32)] * 6,
-            *[pltpu.VMEM((YWIN, TILES, TILE, BLK), bf16)] * 2,
+            *[pltpu.VMEM((rows, columns), f32)] * 4,
             pltpu.VMEM((COLB, TILES, TILE, BLK), bf16),
-            *[pltpu.VMEM((PIECES * TILES, TILE, BLK), bf16)] * 5,
+            pltpu.VMEM((YWIN, TILES, TILE, BLK), bf16),
+            pltpu.VMEM((WIN, BLK, BLK), f32),
+            *[pltpu.VMEM((PIECES * TILES, TILE, BLK), bf16)] * 4,
             *[pltpu.VMEM((4, COLB, TILES, TILE, BLK), bf16)] * 2,
             pltpu.VMEM((WIN, 2, BLK, BLK), bf16),
             pltpu.VMEM((COLB, 2, BLK, BLK), bf16),
             pltpu.VMEM((WIN, BLK, 2 * BLK), bf16),
             pltpu.VMEM((COLB, BLK, 2 * BLK), bf16),
             dma((8,)),
-            dma((2,)),
             *[dma((2, 4))] * 4,
-            dma((2, 2, 4)),
+            dma((1 + len(PARTS), 2, 4)),
             dma((4,)),
+            *[pltpu.VMEM((YWIN, tiles, TILE, BLK), bf16) for _, tiles in PARTS],
+            *[pltpu.VMEM((COLB, tiles, TILE, BLK), bf16) for _, tiles in PARTS],
         ],
         compiler_params=pltpu.CompilerParams(
             collective_id=0, has_side_effects=True, vmem_limit_bytes=60 * 1024 * 1024
@@ -435,10 +444,10 @@
     return pl.pallas_call(
         hand_over,
         out_shape=[jax.ShapeDtypeStruct((rows, columns), f32)] * 2,
-        in_specs=[hbm, hbm],
+        in_specs=[pl.BlockSpec(memory_space=pl.ANY)] * 2,
         out_specs=[hbm, hbm],
-        scratch_shapes=[pltpu.VMEM((2, rows, columns), f32), dma((2, 2))],
-        compiler_params=pltpu.CompilerParams(vmem_limit_bytes=60 * 1024 * 1024),
+        scratch_shapes=[dma((2,))],
+        compiler_params=pltpu.CompilerParams(vmem_limit_bytes=1024 * 1024),
         name="hand_over",
     )(next_vector, after_vector)
 

time: 35.4 us -> 32.8 us (0.927)
  Pallas kernels: 34.5 us -> 32 us
    pallas_call x1, Pallas kernels: 32.9 us -> 31.3 us  [on_device(): pl.pallas_call(kernel, out_shape=[pltpu.VMEM((rows, columns), f32)] * 2,...]
    pallas_call x1, Pallas kernels: 1.68 us -> 0.73 us  [on_device(): pl.pallas_call(hand_over, out_shape=[jax.ShapeDtypeStruct((rows, columns)...]
where the time goes in v4:
time: 32.8 us; the launch traced here: 32.7 us
  Pallas kernels  32 us (98%)
  between operations  0.64 us (2%)
    pallas_call x1, Pallas kernels, on_device(): pl.pallas_call(kernel, out_shape=[pltpu.VMEM((rows, columns), f32)] * 2,...  31.3 us
    pallas_call x1, Pallas kernels, on_device(): pl.pallas_call(hand_over, out_shape=[jax.ShapeDtypeStruct((rows, columns)...  0.73 us

profile of v4, /device:TPU:81, one launch (start us, length us, event | category | flops | bytes accessed | tf_op | source)
XLA Modules:
  0.0 32.7 jit_solution(2073905264730026796)
XLA Ops:
  0.6 31.3 %chebyshev_steps.1 = (f32[48,768]{1,0:T(8,128)S(1)}, f32[48,768]{1,0:T(8,128)S(1)}) custom-call(f32[48,768]{1,0:T(8,128)} %prev_hbm.1, f32[48,768]{1,0:T(8,128)} %this_hbm.1, f32[48,768]{1,0:T(8,128)} %diag_hbm.1, bf16[36,2,128,128]{3,2,1,0:T(8,128)(2,1)} %ablk_hbm.1, s32[8]{0:T(128)} %acls.1, s32[2,36]{1,0:T(2,128)} %bitcast.4, s32[2,36]{1,0:T(2,128)} %bitcast.5, ...), custom_call_target="tpu_custom_call" | custom-call | tf_op jit(solution)/shard_map/chebyshev_steps/pallas_call | solution.py:416
  31.9 0.7 %hand_over.1 = (f32[48,768]{1,0:T(8,128)}, f32[48,768]{1,0:T(8,128)}) custom-call(f32[48,768]{1,0:T(8,128)S(1)} %get-tuple-element.4.next_in, f32[48,768]{1,0:T(8,128)S(1)} %get-tuple-element.5.after_in), custom_call_target="tpu_custom_call" | custom-call | tf_op jit(solution)/shard_map/hand_over/pallas_call | solution.py:444

commit v5 on v4

--- a/solution.py
+++ b/solution.py
@@ -17,7 +17,8 @@
 TILE = 16
 TILES = 3
 PARTS = ((0, 1), (1, 1), (2, 1))
-PIECES = 27
+BTILES = 8
+FAR = 72
 YWIN = 24
 NCLS = 8
 MESH = pl.DeviceIdType.MESH
@@ -71,11 +72,21 @@
     z = lax.div(aa, PLANE)
     p = lax.rem(aa, PLANE)
     is_home = p >= HOME
-    reaches = p < ROWB
+    odd = lax.rem(p, 2) == 1
     has_plane = {d: (z >= -d) if d < 0 else (z < PLANES - d) for d in (-2, -1, 1, 2)}
     has_line = {d: (y >= -d) if d < 0 else (y < LINE - d) for d in (-2, -1, 1, 2)}
-    sends_far = jnp.logical_and(reaches, has_plane[-2])
-    homes_far = jnp.logical_and(is_home, has_plane[2])
+    sides = ((-2, 0, 0, 0), (2, 1, PLANE - ROWB, 1))
+    in_far = {
+        d: jnp.logical_and(p < ROWB if parity == 0 else p >= PLANE - ROWB, has_plane[d])
+        for d, parity, _, _ in sides
+    }
+    home_far = {
+        d: jnp.logical_and(jnp.logical_and(is_home, odd if parity else jnp.logical_not(odd)), has_plane[-d])
+        for d, parity, _, _ in sides
+    }
+
+    def far_tiles(q, skip):
+        return [(k, TILES * q + k - skip) for k in range(TILES) if 0 <= TILES * q + k - skip < BTILES]
 
     def at(d, q):
         return {"aa": aa + (d * PLANE - p) + q, "ba": y}
@@ -107,32 +118,32 @@
     for q in range(1, PLANE):
         greet(at(0, lax.rem(p + q, PLANE)))
 
-    @pl.when(sends_far)
-    def _():
-        for cb in range(COLB):
-            greet(at(-2, HOME + cb))
-
-    @pl.when(homes_far)
-    def _():
-        for q in range(ROWB):
-            greet(at(2, q))
+    for d, parity, low, _ in sides:
+
+        @pl.when(in_far[d])
+        def _(d=d, parity=parity):
+            for cb in range(parity, COLB, 2):
+                greet(at(d, HOME + cb))
+
+        @pl.when(home_far[d])
+        def _(d=d, low=low):
+            for q in range(ROWB):
+                greet(at(-d, low + q))
 
     loads += [
         pltpu.make_async_copy(diag_hbm, dv, load_sem.at[1]),
         pltpu.make_async_copy(prev_hbm, pv, load_sem.at[2]),
         pltpu.make_async_copy(bblk_hbm.at[pl.ds(y * COLB, COLB)], braw, load_sem.at[3]),
     ]
-    for k, (d, count) in enumerate(((-1, ROWB), (0, ROWB), (1, ROWB), (2, 1))):
-        held = lax.rem(z + d + PLANES, PLANES)
+    blocks = PLANES * ROWB
+    a_block = [lax.rem(z * ROWB - ROWB + j + blocks, blocks) for j in range(WIN - 1)]
+    a_block.append(lax.rem(z * ROWB + jnp.where(odd, blocks - 4, 2 * ROWB), blocks))
+    for k, (j, count) in enumerate(((0, ROWB), (ROWB, ROWB), (2 * ROWB, ROWB), (3 * ROWB, 1))):
         loads.append(
             pltpu.make_async_copy(
-                ablk_hbm.at[pl.ds(held * ROWB, count)],
-                araw.at[pl.ds(ROWB * k, count)],
-                load_sem.at[4 + k],
+                ablk_hbm.at[pl.ds(a_block[j], count)], araw.at[pl.ds(j, count)], load_sem.at[4 + k]
             )
         )
-    for c in loads[1:]:
-        c.start()
 
     loads[0].wait()
     for cb in range(COLB):
@@ -141,7 +152,9 @@
         for k, (tile, tiles) in enumerate(PARTS):
             yw0[k][9 + cb] = own[tile : tile + tiles]
 
-    greetings = PLANE - 1 + jnp.where(sends_far, COLB, 0) + jnp.where(homes_far, ROWB, 0)
+    greetings = PLANE - 1
+    for d, _, _, _ in sides:
+        greetings = greetings + jnp.where(in_far[d], COLB // 2, 0) + jnp.where(home_far[d], ROWB, 0)
     for d in (-2, -1, 1, 2):
         greetings = greetings + jnp.where(has_line[d], 1, 0)
     for d in (-1, 1):
@@ -179,12 +192,19 @@
         def place(k):
             return w.at[pl.ds(TILES * k + tile, tiles)]
 
-        @pl.when(sends_far)
-        def _():
-            remote(
-                src, place(3 * PLANE + p),
-                in_send.at[step, 3], in_recv.at[step, 3], at(-2, to),
-            ).start()
+        d, _, low, skip = sides[cb % 2]
+
+        for q in range(ROWB):
+            spots = [(k, spot) for k, spot in far_tiles(q, skip) if tile <= k < tile + tiles]
+            if spots:
+
+                @pl.when(jnp.logical_and(p == low + q, has_plane[d]))
+                def _(spots=spots):
+                    remote(
+                        src.at[pl.ds(spots[0][0] - tile, len(spots))],
+                        w.at[pl.ds(FAR + spots[0][1], len(spots))],
+                        in_send.at[step, 3], in_recv.at[step, 3], at(d, to),
+                    ).start()
 
         for k, d, base in ((2, -1, 2 * PLANE), (0, 1, 0)):
 
@@ -208,8 +228,21 @@
     def await_pieces(count, sem):
         await_bytes(win0.at[pl.ds(0, count * TILES)], sem)
 
+    def await_far_rows(sem):
+        for d, _, low, skip in sides:
+            for q in range(ROWB):
+                count = COLB // 2 * len(far_tiles(q, skip))
+
+                @pl.when(jnp.logical_and(p == low + q, has_plane[d]))
+                def _(count=count):
+                    await_bytes(win0.at[pl.ds(0, count)], sem)
+
+    def await_far_block(sem):
+        for d, _, _, _ in sides:
+            pl.when(home_far[d])(lambda: await_bytes(win0.at[pl.ds(0, BTILES)], sem))
+
     def sent_in(step):
-        pl.when(sends_far)(lambda: await_pieces(COLB, in_send.at[step, 3]))
+        await_far_rows(in_send.at[step, 3])
         pl.when(has_plane[-1])(lambda: await_pieces(COLB, in_send.at[step, 2]))
         pl.when(has_plane[1])(lambda: await_pieces(COLB, in_send.at[step, 0]))
         pl.when(is_home)(lambda: await_pieces(COLB - 1, in_send.at[step, 1]))
@@ -220,12 +253,25 @@
         await_pieces(PLANE - 1, in_recv.at[step, 1])
         pl.when(has_plane[-1])(lambda: await_pieces(PLANE, in_recv.at[step, 0]))
         pl.when(has_plane[1])(lambda: await_pieces(PLANE, in_recv.at[step, 2]))
-        pl.when(has_plane[2])(lambda: await_pieces(ROWB, in_recv.at[step, 3]))
-
-    def send_out(src, rec, step, d, base, slot, count):
+        await_far_block(in_recv.at[step, 3])
+
+    def send_far(src, rec, step):
+        for d, _, low, skip in sides:
+
+            @pl.when(home_far[d])
+            def _(d=d, low=low, skip=skip):
+                for q in range(ROWB):
+                    spots = far_tiles(q, skip)
+                    remote(
+                        src.at[pl.ds(FAR + spots[0][1], len(spots))],
+                        rec.at[3, p - HOME, pl.ds(spots[0][0], len(spots))],
+                        out_send.at[step, 3], out_recv.at[step, 3], at(-d, low + q),
+                    ).start()
+
+    def send_out(src, rec, step, d, base, slot):
         @pl.when(has_plane[d])
         def _():
-            for q in range(count):
+            for q in range(PLANE):
                 remote(
                     src.at[piece(base + q)], rec.at[slot, p - HOME],
                     out_send.at[step, slot], out_recv.at[step, slot], at(d, q),
@@ -244,12 +290,12 @@
 
     def sent_out(step):
         await_pieces(PLANE - 1, out_send.at[step, 1])
-        pl.when(has_plane[2])(lambda: await_pieces(ROWB, out_send.at[step, 3]))
+        await_far_block(out_send.at[step, 3])
         pl.when(has_plane[1])(lambda: await_pieces(PLANE, out_send.at[step, 0]))
         pl.when(has_plane[-1])(lambda: await_pieces(PLANE, out_send.at[step, 2]))
 
     def arrived_out(step):
-        pl.when(sends_far)(lambda: await_pieces(COLB, out_recv.at[step, 3]))
+        await_far_rows(out_recv.at[step, 3])
         pl.when(has_plane[-1])(lambda: await_pieces(COLB, out_recv.at[step, 0]))
         pl.when(has_plane[1])(lambda: await_pieces(COLB, out_recv.at[step, 2]))
         pl.when(jnp.logical_not(is_home))(lambda: await_pieces(COLB, out_recv.at[step, 1]))
@@ -263,21 +309,19 @@
         y_start(yw0[k], k)
     for cb in range(COLB):
         send_in(xb.at[cb], win0, 0, cb, 0, TILES)
+    for c in loads[1:]:
+        c.start()
 
     a_table = class_table(acls)
     b_table = class_table(bcls)
     a_at = []
     for j in range(WIN):
-        block = lax.rem(z * ROWB - ROWB + j + PLANES * ROWB, PLANES * ROWB)
-        start, length = class_of(block, a_table)
-        a_at.append(
-            [
-                jnp.clip(
-                    column_of(start, length, aoff[k, block], 3) - (z - 1) * ROWB, 0, WIN - 1
-                )
-                for k in range(2)
-            ]
-        )
+        start, length = class_of(a_block[j], a_table)
+        spots = []
+        for k in range(2):
+            spot = column_of(start, length, aoff[k, a_block[j]], 3) - (z - 1) * ROWB
+            spots.append(jnp.where(spot < 0, WIN - 1, jnp.minimum(spot, WIN - 1)))
+        a_at.append(spots)
     b_at = []
     for r in range(COLB):
         block = y * COLB + r
@@ -291,11 +335,14 @@
             ]
         )
     slot_at = []
-    for q in range(3):
-        start, length = class_of(z * ROWB + lax.div(3 * p + q, PLANE), a_table)
-        middle = start + lax.div(length - 1, 2)
-        away = lax.div(middle, ROWB) - z
-        slot_at.append(jnp.clip(jnp.where(away == -2, 3, away + 1), 0, 3))
+    for parity in range(2):
+        slots = []
+        for q in range(TILES):
+            start, length = class_of(z * ROWB + lax.div(TILES * p + q, PLANE), a_table)
+            away = lax.div(start + lax.div(length - 1 + parity, 2), ROWB) - z
+            slot = jnp.where(jnp.logical_or(away < -1, away > 1), 3, away + 1)
+            slots.append(jnp.clip(slot, 0, 3))
+        slot_at.append(slots)
 
     for c in loads[1:]:
         c.wait()
@@ -309,14 +356,11 @@
     @pl.when(is_home)
     def _():
         for j in range(WIN):
-            block = lax.rem(z * ROWB - ROWB + j + PLANES * ROWB, PLANES * ROWB)
             for k in range(2):
-                live = amask[k, block].astype(jnp.float32)
+                live = amask[k, a_block[j]].astype(jnp.float32)
                 aw[j, :, k * BLK : (k + 1) * BLK] = (
                     araw[j, k].astype(jnp.float32) * live
                 ).astype(jnp.bfloat16)
-        al0[8 * WIN] = jnp.zeros((TILE, BLK), jnp.bfloat16)
-        al1[8 * WIN] = jnp.zeros((TILE, BLK), jnp.bfloat16)
 
     def beta(w, r, rows):
         both = jnp.concatenate([w[b_at[r][k]].reshape(rows, BLK) for k in range(2)], axis=1)
@@ -339,17 +383,17 @@
 
     def alpha_and_send(w, out, rec, step, more):
         alpha(w, out, range(9, 10), more)
-        send_out(out, rec, step, 2, 3 * PLANE, 3, ROWB)
+        send_far(out, rec, step)
         alpha(w, out, range(6, 9), more)
-        send_out(out, rec, step, 1, 2 * PLANE, 0, PLANE)
+        send_out(out, rec, step, 1, 2 * PLANE, 0)
         alpha(w, out, range(0, 3), more)
-        send_out(out, rec, step, -1, 0, 2, PLANE)
+        send_out(out, rec, step, -1, 0, 2)
         alpha(w, out, range(3, 6), more)
         send_own(out, rec, step)
 
     def returned(rec, cb):
         return jnp.concatenate(
-            [rec[slot_at[q], cb, q] for q in range(TILES)], axis=0
+            [rec[slot_at[cb % 2][q], cb, q] for q in range(TILES)], axis=0
         ).astype(jnp.float32)
 
     for k, (tile, tiles) in enumerate(PARTS):
@@ -423,7 +467,7 @@
             pltpu.VMEM((COLB, TILES, TILE, BLK), bf16),
             pltpu.VMEM((YWIN, TILES, TILE, BLK), bf16),
             pltpu.VMEM((WIN, BLK, BLK), f32),
-            *[pltpu.VMEM((PIECES * TILES, TILE, BLK), bf16)] * 4,
+            *[pltpu.VMEM((WIN * BTILES, TILE, BLK), bf16)] * 4,
             *[pltpu.VMEM((4, COLB, TILES, TILE, BLK), bf16)] * 2,
             pltpu.VMEM((WIN, 2, BLK, BLK), bf16),
             pltpu.VMEM((COLB, 2, BLK, BLK), bf16),

time: 32.8 us -> 32.3 us (0.985)
  the two profiles are of different devices: /device:TPU:81 before, /device:TPU:145 now
where the time goes in v5:
time: 32.3 us; the launch traced here: 32.1 us
  Pallas kernels  31.5 us (98%)
  between operations  0.64 us (2%)
    pallas_call x1, Pallas kernels, on_device(): pl.pallas_call(kernel, out_shape=[pltpu.VMEM((rows, columns), f32)] * 2,...  30.8 us
    pallas_call x1, Pallas kernels, on_device(): pl.pallas_call(hand_over, out_shape=[jax.ShapeDtypeStruct((rows, columns)...  0.73 us

profile of v5, /device:TPU:145, one launch (start us, length us, event | category | flops | bytes accessed | tf_op | source)
XLA Modules:
  0.0 32.1 jit_solution(15238661228836566388)
XLA Ops:
  0.6 30.8 %chebyshev_steps.1 = (f32[48,768]{1,0:T(8,128)S(1)}, f32[48,768]{1,0:T(8,128)S(1)}) custom-call(f32[48,768]{1,0:T(8,128)} %prev_hbm.1, f32[48,768]{1,0:T(8,128)} %this_hbm.1, f32[48,768]{1,0:T(8,128)} %diag_hbm.1, bf16[36,2,128,128]{3,2,1,0:T(8,128)(2,1)} %ablk_hbm.1, s32[8]{0:T(128)} %acls.1, s32[2,36]{1,0:T(2,128)} %bitcast.4, s32[2,36]{1,0:T(2,128)} %bitcast.5, ...), custom_call_target="tpu_custom_call" | custom-call | tf_op jit(solution)/shard_map/chebyshev_steps/pallas_call | solution.py:460
  31.4 0.7 %hand_over.1 = (f32[48,768]{1,0:T(8,128)}, f32[48,768]{1,0:T(8,128)}) custom-call(f32[48,768]{1,0:T(8,128)S(1)} %get-tuple-element.4.next_in, f32[48,768]{1,0:T(8,128)S(1)} %get-tuple-element.5.after_in), custom_call_target="tpu_custom_call" | custom-call | tf_op jit(solution)/shard_map/hand_over/pallas_call | solution.py:488

commit v6 on v5

--- a/solution.py
+++ b/solution.py
@@ -145,6 +145,9 @@
             )
         )
 
+    for c in loads[1:]:
+        c.start()
+
     loads[0].wait()
     for cb in range(COLB):
         own = xv[:, cb * BLK : (cb + 1) * BLK].astype(jnp.bfloat16).reshape(TILES, TILE, BLK)
@@ -152,176 +155,7 @@
         for k, (tile, tiles) in enumerate(PARTS):
             yw0[k][9 + cb] = own[tile : tile + tiles]
 
-    greetings = PLANE - 1
-    for d, _, _, _ in sides:
-        greetings = greetings + jnp.where(in_far[d], COLB // 2, 0) + jnp.where(home_far[d], ROWB, 0)
-    for d in (-2, -1, 1, 2):
-        greetings = greetings + jnp.where(has_line[d], 1, 0)
-    for d in (-1, 1):
-        greetings = greetings + jnp.where(has_plane[d], PLANE, 0)
-    pl.semaphore_wait(barrier, greetings)
-
-    def y_copy(w, at_sem, k):
-        src, n, dst, d = ((9, 6, 3, 1), (9, 6, 15, -1), (12, 3, 0, 2), (9, 3, 21, -2))[k]
-        return d, remote(
-            w.at[pl.ds(src, n)], w.at[pl.ds(dst, n)],
-            y_sem.at[at_sem, 0, k], y_sem.at[at_sem, 1, k], along(d),
-        )
-
-    def y_start(w, at_sem):
-        for k in range(4):
-            d, copy = y_copy(w, at_sem, k)
-            pl.when(has_line[d])(copy.start)
-
-    def y_sent(w, at_sem):
-        for k in range(4):
-            d, copy = y_copy(w, at_sem, k)
-            pl.when(has_line[d])(copy.wait_send)
-
-    def y_arrived(w, at_sem):
-        for k in range(4):
-            d, copy = y_copy(w, at_sem, k)
-            pl.when(has_line[-d])(copy.wait_recv)
-
-    def piece(k):
-        return pl.ds(TILES * k, TILES)
-
-    def send_in(src, w, step, cb, tile, tiles):
-        to = HOME + cb
-
-        def place(k):
-            return w.at[pl.ds(TILES * k + tile, tiles)]
-
-        d, _, low, skip = sides[cb % 2]
-
-        for q in range(ROWB):
-            spots = [(k, spot) for k, spot in far_tiles(q, skip) if tile <= k < tile + tiles]
-            if spots:
-
-                @pl.when(jnp.logical_and(p == low + q, has_plane[d]))
-                def _(spots=spots):
-                    remote(
-                        src.at[pl.ds(spots[0][0] - tile, len(spots))],
-                        w.at[pl.ds(FAR + spots[0][1], len(spots))],
-                        in_send.at[step, 3], in_recv.at[step, 3], at(d, to),
-                    ).start()
-
-        for k, d, base in ((2, -1, 2 * PLANE), (0, 1, 0)):
-
-            @pl.when(has_plane[d])
-            def _(k=k, d=d, base=base):
-                remote(
-                    src, place(base + p),
-                    in_send.at[step, k], in_recv.at[step, k], at(d, to),
-                ).start()
-
-        @pl.when(p != to)
-        def _():
-            remote(
-                src, place(PLANE + p), in_send.at[step, 1], in_recv.at[step, 1], at(0, to)
-            ).start()
-
-        @pl.when(p == to)
-        def _():
-            pltpu.make_async_copy(src, place(PLANE + p), self_sem.at[step]).start()
-
-    def await_pieces(count, sem):
-        await_bytes(win0.at[pl.ds(0, count * TILES)], sem)
-
-    def await_far_rows(sem):
-        for d, _, low, skip in sides:
-            for q in range(ROWB):
-                count = COLB // 2 * len(far_tiles(q, skip))
-
-                @pl.when(jnp.logical_and(p == low + q, has_plane[d]))
-                def _(count=count):
-                    await_bytes(win0.at[pl.ds(0, count)], sem)
-
-    def await_far_block(sem):
-        for d, _, _, _ in sides:
-            pl.when(home_far[d])(lambda: await_bytes(win0.at[pl.ds(0, BTILES)], sem))
-
-    def sent_in(step):
-        await_far_rows(in_send.at[step, 3])
-        pl.when(has_plane[-1])(lambda: await_pieces(COLB, in_send.at[step, 2]))
-        pl.when(has_plane[1])(lambda: await_pieces(COLB, in_send.at[step, 0]))
-        pl.when(is_home)(lambda: await_pieces(COLB - 1, in_send.at[step, 1]))
-        pl.when(jnp.logical_not(is_home))(lambda: await_pieces(COLB, in_send.at[step, 1]))
-
-    def arrived_in(step):
-        await_pieces(1, self_sem.at[step])
-        await_pieces(PLANE - 1, in_recv.at[step, 1])
-        pl.when(has_plane[-1])(lambda: await_pieces(PLANE, in_recv.at[step, 0]))
-        pl.when(has_plane[1])(lambda: await_pieces(PLANE, in_recv.at[step, 2]))
-        await_far_block(in_recv.at[step, 3])
-
-    def send_far(src, rec, step):
-        for d, _, low, skip in sides:
-
-            @pl.when(home_far[d])
-            def _(d=d, low=low, skip=skip):
-                for q in range(ROWB):
-                    spots = far_tiles(q, skip)
-                    remote(
-                        src.at[pl.ds(FAR + spots[0][1], len(spots))],
-                        rec.at[3, p - HOME, pl.ds(spots[0][0], len(spots))],
-                        out_send.at[step, 3], out_recv.at[step, 3], at(-d, low + q),
-                    ).start()
-
-    def send_out(src, rec, step, d, base, slot):
-        @pl.when(has_plane[d])
-        def _():
-            for q in range(PLANE):
-                remote(
-                    src.at[piece(base + q)], rec.at[slot, p - HOME],
-                    out_send.at[step, slot], out_recv.at[step, slot], at(d, q),
-                ).start()
-
-    def send_own(src, rec, step):
-        for k in range(1, PLANE):
-            q = lax.rem(p + k, PLANE)
-            remote(
-                src.at[piece(PLANE + q)], rec.at[1, p - HOME],
-                out_send.at[step, 1], out_recv.at[step, 1], at(0, q),
-            ).start()
-        pltpu.make_async_copy(
-            src.at[piece(PLANE + p)], rec.at[1, p - HOME], self_sem.at[2 + step]
-        ).start()
-
-    def sent_out(step):
-        await_pieces(PLANE - 1, out_send.at[step, 1])
-        await_far_block(out_send.at[step, 3])
-        pl.when(has_plane[1])(lambda: await_pieces(PLANE, out_send.at[step, 0]))
-        pl.when(has_plane[-1])(lambda: await_pieces(PLANE, out_send.at[step, 2]))
-
-    def arrived_out(step):
-        await_far_rows(out_recv.at[step, 3])
-        pl.when(has_plane[-1])(lambda: await_pieces(COLB, out_recv.at[step, 0]))
-        pl.when(has_plane[1])(lambda: await_pieces(COLB, out_recv.at[step, 2]))
-        pl.when(jnp.logical_not(is_home))(lambda: await_pieces(COLB, out_recv.at[step, 1]))
-
-        @pl.when(is_home)
-        def _():
-            await_pieces(COLB - 1, out_recv.at[step, 1])
-            await_pieces(1, self_sem.at[2 + step])
-
-    for k in range(len(PARTS)):
-        y_start(yw0[k], k)
-    for cb in range(COLB):
-        send_in(xb.at[cb], win0, 0, cb, 0, TILES)
-    for c in loads[1:]:
-        c.start()
-
-    a_table = class_table(acls)
     b_table = class_table(bcls)
-    a_at = []
-    for j in range(WIN):
-        start, length = class_of(a_block[j], a_table)
-        spots = []
-        for k in range(2):
-            spot = column_of(start, length, aoff[k, a_block[j]], 3) - (z - 1) * ROWB
-            spots.append(jnp.where(spot < 0, WIN - 1, jnp.minimum(spot, WIN - 1)))
-        a_at.append(spots)
     b_at = []
     for r in range(COLB):
         block = y * COLB + r
@@ -334,33 +168,175 @@
                 for k in range(2)
             ]
         )
-    slot_at = []
-    for parity in range(2):
-        slots = []
-        for q in range(TILES):
-            start, length = class_of(z * ROWB + lax.div(TILES * p + q, PLANE), a_table)
-            away = lax.div(start + lax.div(length - 1 + parity, 2), ROWB) - z
-            slot = jnp.where(jnp.logical_or(away < -1, away > 1), 3, away + 1)
-            slots.append(jnp.clip(slot, 0, 3))
-        slot_at.append(slots)
-
-    for c in loads[1:]:
+    greetings = PLANE - 1
+    for d, _, _, _ in sides:
+        greetings = greetings + jnp.where(in_far[d], COLB // 2, 0) + jnp.where(home_far[d], ROWB, 0)
+    for d in (-2, -1, 1, 2):
+        greetings = greetings + jnp.where(has_line[d], 1, 0)
+    for d in (-1, 1):
+        greetings = greetings + jnp.where(has_plane[d], PLANE, 0)
+    pl.semaphore_wait(barrier, greetings)
+
+    def y_copy(w, at_sem, k):
+        src, n, dst, d = ((9, 6, 3, 1), (9, 6, 15, -1), (12, 3, 0, 2), (9, 3, 21, -2))[k]
+        return d, remote(
+            w.at[pl.ds(src, n)], w.at[pl.ds(dst, n)],
+            y_sem.at[at_sem, 0, k], y_sem.at[at_sem, 1, k], along(d),
+        )
+
+    def y_start(w, at_sem):
+        for k in range(4):
+            d, copy = y_copy(w, at_sem, k)
+            pl.when(has_line[d])(copy.start)
+
+    def y_sent(w, at_sem):
+        for k in range(4):
+            d, copy = y_copy(w, at_sem, k)
+            pl.when(has_line[d])(copy.wait_send)
+
+    def y_arrived(w, at_sem):
+        for k in range(4):
+            d, copy = y_copy(w, at_sem, k)
+            pl.when(has_line[-d])(copy.wait_recv)
+
+    def piece(k):
+        return pl.ds(TILES * k, TILES)
+
+    def send_in(src, w, step, tile, tiles):
+        def place(k):
+            return w.at[pl.ds(TILES * k + tile, tiles)]
+
+        for d, parity, low, skip in sides:
+            for q in range(ROWB):
+                spots = [(k, spot) for k, spot in far_tiles(q, skip) if tile <= k < tile + tiles]
+                if spots:
+
+                    @pl.when(jnp.logical_and(p == low + q, has_plane[d]))
+                    def _(d=d, parity=parity, spots=spots):
+                        for cb in range(parity, COLB, 2):
+                            remote(
+                                src.at[cb, pl.ds(spots[0][0] - tile, len(spots))],
+                                w.at[pl.ds(FAR + spots[0][1], len(spots))],
+                                in_send.at[step, 3], in_recv.at[step, 3], at(d, HOME + cb),
+                            ).start()
+
+        for k, d, base in ((2, -1, 2 * PLANE), (0, 1, 0)):
+
+            @pl.when(has_plane[d])
+            def _(k=k, d=d, base=base):
+                for cb in range(COLB):
+                    remote(
+                        src.at[cb], place(base + p),
+                        in_send.at[step, k], in_recv.at[step, k], at(d, HOME + cb),
+                    ).start()
+
+        def to_own(cb):
+            remote(
+                src.at[cb], place(PLANE + p),
+                in_send.at[step, 1], in_recv.at[step, 1], at(0, HOME + cb),
+            ).start()
+
+        @pl.when(is_home)
+        def _():
+            for k in range(1, COLB):
+                to_own(lax.rem(p - HOME + k, COLB))
+            pltpu.make_async_copy(src.at[p - HOME], place(PLANE + p), self_sem.at[step]).start()
+
+        @pl.when(jnp.logical_not(is_home))
+        def _():
+            for cb in range(COLB):
+                to_own(cb)
+
+    def await_pieces(count, sem):
+        await_bytes(win0.at[pl.ds(0, count * TILES)], sem)
+
+    def await_far_rows(sem):
+        for d, _, low, skip in sides:
+            for q in range(ROWB):
+                count = COLB // 2 * len(far_tiles(q, skip))
+
+                @pl.when(jnp.logical_and(p == low + q, has_plane[d]))
+                def _(count=count):
+                    await_bytes(win0.at[pl.ds(0, count)], sem)
+
+    def await_far_block(sem):
+        for d, _, _, _ in sides:
+            pl.when(home_far[d])(lambda: await_bytes(win0.at[pl.ds(0, BTILES)], sem))
+
+    def sent_in(step):
+        await_far_rows(in_send.at[step, 3])
+        pl.when(has_plane[-1])(lambda: await_pieces(COLB, in_send.at[step, 2]))
+        pl.when(has_plane[1])(lambda: await_pieces(COLB, in_send.at[step, 0]))
+        pl.when(is_home)(lambda: await_pieces(COLB - 1, in_send.at[step, 1]))
+        pl.when(jnp.logical_not(is_home))(lambda: await_pieces(COLB, in_send.at[step, 1]))
+
+    def arrived_in(step):
+        await_pieces(1, self_sem.at[step])
+        await_pieces(PLANE - 1, in_recv.at[step, 1])
+        pl.when(has_plane[-1])(lambda: await_pieces(PLANE, in_recv.at[step, 0]))
+        pl.when(has_plane[1])(lambda: await_pieces(PLANE, in_recv.at[step, 2]))
+        await_far_block(in_recv.at[step, 3])
+
+    def send_far(src, rec, step):
+        for d, _, low, skip in sides:
+
+            @pl.when(home_far[d])
+            def _(d=d, low=low, skip=skip):
+                for q in range(ROWB):
+                    spots = far_tiles(q, skip)
+                    remote(
+                        src.at[pl.ds(FAR + spots[0][1], len(spots))],
+                        rec.at[3, p - HOME, pl.ds(spots[0][0], len(spots))],
+                        out_send.at[step, 3], out_recv.at[step, 3], at(-d, low + q),
+                    ).start()
+
+    def send_out(src, rec, step, d, base, slot):
+        @pl.when(has_plane[d])
+        def _():
+            for q in range(PLANE):
+                remote(
+                    src.at[piece(base + q)], rec.at[slot, p - HOME],
+                    out_send.at[step, slot], out_recv.at[step, slot], at(d, q),
+                ).start()
+
+    def send_own(src, rec, step):
+        for k in range(1, PLANE):
+            q = lax.rem(p + k, PLANE)
+            remote(
+                src.at[piece(PLANE + q)], rec.at[1, p - HOME],
+                out_send.at[step, 1], out_recv.at[step, 1], at(0, q),
+            ).start()
+        pltpu.make_async_copy(
+            src.at[piece(PLANE + p)], rec.at[1, p - HOME], self_sem.at[2 + step]
+        ).start()
+
+    def sent_out(step):
+        await_pieces(PLANE - 1, out_send.at[step, 1])
+        await_far_block(out_send.at[step, 3])
+        pl.when(has_plane[1])(lambda: await_pieces(PLANE, out_send.at[step, 0]))
+        pl.when(has_plane[-1])(lambda: await_pieces(PLANE, out_send.at[step, 2]))
+
+    def arrived_out(step):
+        await_far_rows(out_recv.at[step, 3])
+        pl.when(has_plane[-1])(lambda: await_pieces(COLB, out_recv.at[step, 0]))
+        pl.when(has_plane[1])(lambda: await_pieces(COLB, out_recv.at[step, 2]))
+        pl.when(jnp.logical_not(is_home))(lambda: await_pieces(COLB, out_recv.at[step, 1]))
+
+        @pl.when(is_home)
+        def _():
+            await_pieces(COLB - 1, out_recv.at[step, 1])
+            await_pieces(1, self_sem.at[2 + step])
+
+    for k in range(len(PARTS)):
+        y_start(yw0[k], k)
+    send_in(xb, win0, 0, 0, TILES)
+
+    for c in loads[1:4]:
         c.wait()
     for r in range(COLB):
         for k in range(2):
-            live = bmask[k, y * COLB + r].astype(jnp.float32)
-            bw[r, :, k * BLK : (k + 1) * BLK] = (braw[r, k].astype(jnp.float32) * live).astype(
-                jnp.bfloat16
-            )
-
-    @pl.when(is_home)
-    def _():
-        for j in range(WIN):
-            for k in range(2):
-                live = amask[k, a_block[j]].astype(jnp.float32)
-                aw[j, :, k * BLK : (k + 1) * BLK] = (
-                    araw[j, k].astype(jnp.float32) * live
-                ).astype(jnp.bfloat16)
+            live = jnp.full((BLK, BLK), bmask[k, y * COLB + r].astype(jnp.float32))
+            bw[r, :, k * BLK : (k + 1) * BLK] = braw[r, k] * live.astype(jnp.bfloat16)
 
     def beta(w, r, rows):
         both = jnp.concatenate([w[b_at[r][k]].reshape(rows, BLK) for k in range(2)], axis=1)
@@ -389,6 +365,12 @@
         alpha(w, out, range(0, 3), more)
         send_out(out, rec, step, -1, 0, 2)
         alpha(w, out, range(3, 6), more)
+        send_own(out, rec, step)
+
+    def send_all(out, rec, step):
+        send_far(out, rec, step)
+        send_out(out, rec, step, 1, 2 * PLANE, 0)
+        send_out(out, rec, step, -1, 0, 2)
         send_own(out, rec, step)
 
     def returned(rec, cb):
@@ -406,15 +388,46 @@
             tv[rows, cols] = t
             yw1[9 + cb, tile : tile + tiles] = t.astype(jnp.bfloat16).reshape(tiles, TILE, BLK)
             tb[k][cb] = (t + 2.0 * b1).astype(jnp.bfloat16).reshape(tiles, TILE, BLK)
-            send_in(tb[k].at[cb], wint, 1, cb, tile, tiles)
+        send_in(tb[k], wint, 1, tile, tiles)
     y_start(yw1, len(PARTS))
+
+    a_table = class_table(acls)
+    a_at = []
+    for j in range(WIN):
+        start, length = class_of(a_block[j], a_table)
+        spots = []
+        for k in range(2):
+            spot = column_of(start, length, aoff[k, a_block[j]], 3) - (z - 1) * ROWB
+            spots.append(jnp.where(spot < 0, WIN - 1, jnp.minimum(spot, WIN - 1)))
+        a_at.append(spots)
+    slot_at = []
+    for parity in range(2):
+        slots = []
+        for q in range(TILES):
+            start, length = class_of(z * ROWB + lax.div(TILES * p + q, PLANE), a_table)
+            away = lax.div(start + lax.div(length - 1 + parity, 2), ROWB) - z
+            slot = jnp.where(jnp.logical_or(away < -1, away > 1), 3, away + 1)
+            slots.append(jnp.clip(slot, 0, 3))
+        slot_at.append(slots)
+
+    for c in loads[4:]:
+        c.wait()
+
+    @pl.when(is_home)
+    def _():
+        for j in range(WIN):
+            for k in range(2):
+                live = jnp.full((BLK, BLK), amask[k, a_block[j]].astype(jnp.float32))
+                aw[j, :, k * BLK : (k + 1) * BLK] = araw[j, k] * live.astype(jnp.bfloat16)
+
 
     @pl.when(is_home)
     def _():
         arrived_in(0)
-        alpha_and_send(win0, al0, rec0, 0, False)
+        alpha(win0, al0, range(WIN), False)
         for j in range(WIN):
             pre[j] = 2.0 * couple(al0, j)
+        send_all(al0, rec0, 0)
         arrived_in(1)
         alpha_and_send(wint, al1, rec1, 1, True)
 

time: 32.3 us -> 31.5 us (0.975)
  the two profiles are of different devices: /device:TPU:145 before, /device:TPU:81 now
where the time goes in v6:
time: 31.5 us; the launch traced here: 31.3 us
  Pallas kernels  30.6 us (97%)
  between operations  0.64 us (2%)
    pallas_call x1, Pallas kernels, on_device(): pl.pallas_call(kernel, out_shape=[pltpu.VMEM((rows, columns), f32)] * 2,...  29.9 us
    pallas_call x1, Pallas kernels, on_device(): pl.pallas_call(hand_over, out_shape=[jax.ShapeDtypeStruct((rows, columns)...  0.73 us

profile of v6, /device:TPU:81, one launch (start us, length us, event | category | flops | bytes accessed | tf_op | source)
XLA Modules:
  0.0 31.3 jit_solution(9329286370975402184)
XLA Ops:
  0.6 29.9 %chebyshev_steps.1 = (f32[48,768]{1,0:T(8,128)S(1)}, f32[48,768]{1,0:T(8,128)S(1)}) custom-call(f32[48,768]{1,0:T(8,128)} %prev_hbm.1, f32[48,768]{1,0:T(8,128)} %this_hbm.1, f32[48,768]{1,0:T(8,128)} %diag_hbm.1, bf16[36,2,128,128]{3,2,1,0:T(8,128)(2,1)} %ablk_hbm.1, s32[8]{0:T(128)} %acls.1, s32[2,36]{1,0:T(2,128)} %bitcast.4, s32[2,36]{1,0:T(2,128)} %bitcast.5, ...), custom_call_target="tpu_custom_call" | custom-call | tf_op jit(solution)/shard_map/chebyshev_steps/pallas_call | solution.py:473
  30.5 0.7 %hand_over.1 = (f32[48,768]{1,0:T(8,128)}, f32[48,768]{1,0:T(8,128)}) custom-call(f32[48,768]{1,0:T(8,128)S(1)} %get-tuple-element.4.next_in, f32[48,768]{1,0:T(8,128)S(1)} %get-tuple-element.5.after_in), custom_call_target="tpu_custom_call" | custom-call | tf_op jit(solution)/shard_map/hand_over/pallas_call | solution.py:501

commit v7 on v6

--- a/solution.py
+++ b/solution.py
@@ -439,17 +439,16 @@
     for cb in range(COLB):
         cols = slice(cb * BLK, (cb + 1) * BLK)
         tv[:, cols] = 2.0 * (beta(yw1, cb, ROWS) + dv[:, cols] * nv[:, cols]) - xv[:, cols]
-    arrived_out(1)
-    for cb in range(COLB):
-        cols = slice(cb * BLK, (cb + 1) * BLK)
-        ov[:, cols] = tv[:, cols] + 2.0 * returned(rec1, cb)
-
     for step in range(2):
         sent_in(step)
         pl.when(is_home)(lambda step=step: sent_out(step))
     for k in range(len(PARTS)):
         y_sent(yw0[k], k)
     y_sent(yw1, len(PARTS))
+    arrived_out(1)
+    for cb in range(COLB):
+        cols = slice(cb * BLK, (cb + 1) * BLK)
+        ov[:, cols] = tv[:, cols] + 2.0 * returned(rec1, cb)
 
 
 def hand_over(next_in, after_in, next_out, after_out, sem):

time: 31.5 us -> 31.4 us (level)
  no operation moved by 1% of the time
where the time goes in v7:
time: 31.4 us; the launch traced here: 31.2 us
  Pallas kernels  30.6 us (97%)
  between operations  0.64 us (2%)
    pallas_call x1, Pallas kernels, on_device(): pl.pallas_call(kernel, out_shape=[pltpu.VMEM((rows, columns), f32)] * 2,...  29.8 us
    pallas_call x1, Pallas kernels, on_device(): pl.pallas_call(hand_over, out_shape=[jax.ShapeDtypeStruct((rows, columns)...  0.73 us

profile of v7, /device:TPU:81, one launch (start us, length us, event | category | flops | bytes accessed | tf_op | source)
XLA Modules:
  0.0 31.2 jit_solution(9829205825513686552)
XLA Ops:
  0.6 29.8 %chebyshev_steps.1 = (f32[48,768]{1,0:T(8,128)S(1)}, f32[48,768]{1,0:T(8,128)S(1)}) custom-call(f32[48,768]{1,0:T(8,128)} %prev_hbm.1, f32[48,768]{1,0:T(8,128)} %this_hbm.1, f32[48,768]{1,0:T(8,128)} %diag_hbm.1, bf16[36,2,128,128]{3,2,1,0:T(8,128)(2,1)} %ablk_hbm.1, s32[8]{0:T(128)} %acls.1, s32[2,36]{1,0:T(2,128)} %bitcast.4, s32[2,36]{1,0:T(2,128)} %bitcast.5, ...), custom_call_target="tpu_custom_call" | custom-call | tf_op jit(solution)/shard_map/chebyshev_steps/pallas_call | solution.py:472
  30.5 0.7 %hand_over.1 = (f32[48,768]{1,0:T(8,128)}, f32[48,768]{1,0:T(8,128)}) custom-call(f32[48,768]{1,0:T(8,128)S(1)} %get-tuple-element.4.next_in, f32[48,768]{1,0:T(8,128)S(1)} %get-tuple-element.5.after_in), custom_call_target="tpu_custom_call" | custom-call | tf_op jit(solution)/shard_map/hand_over/pallas_call | solution.py:500

commit v8 on v7

--- a/solution.py
+++ b/solution.py
@@ -64,7 +64,7 @@
     prev_hbm, this_hbm, diag_hbm, ablk_hbm, acls, aoff, amask, bblk_hbm, bcls, boff, bmask,
     nv, ov,
     xv, pv, dv, tv, xb, yw1, pre, win0, wint, al0, al1, rec0, rec1, araw, braw, aw, bw,
-    load_sem, in_send, in_recv, out_send, out_recv, y_sem, self_sem, *parts,
+    load_sem, x_sem, in_send, in_recv, out_send, out_recv, y_sem, self_sem, *parts,
 ):
     yw0, tb = parts[: len(PARTS)], parts[len(PARTS) :]
     aa = lax.axis_index("aa")
@@ -94,8 +94,14 @@
     def along(d):
         return {"aa": aa, "ba": y + d}
 
-    loads = [pltpu.make_async_copy(this_hbm, xv, load_sem.at[0])]
-    loads[0].start()
+    x_loads = [
+        pltpu.make_async_copy(
+            this_hbm.at[pl.ds(TILE * k, TILE)], xv.at[pl.ds(TILE * k, TILE)], x_sem.at[k]
+        )
+        for k in range(TILES)
+    ]
+    for c in x_loads:
+        c.start()
 
     barrier = pltpu.get_barrier_semaphore()
 
@@ -130,7 +136,7 @@
             for q in range(ROWB):
                 greet(at(-d, low + q))
 
-    loads += [
+    loads = [
         pltpu.make_async_copy(diag_hbm, dv, load_sem.at[1]),
         pltpu.make_async_copy(prev_hbm, pv, load_sem.at[2]),
         pltpu.make_async_copy(bblk_hbm.at[pl.ds(y * COLB, COLB)], braw, load_sem.at[3]),
@@ -145,10 +151,11 @@
             )
         )
 
-    for c in loads[1:]:
+    for c in loads:
         c.start()
 
-    loads[0].wait()
+    for c in x_loads:
+        c.wait()
     for cb in range(COLB):
         own = xv[:, cb * BLK : (cb + 1) * BLK].astype(jnp.bfloat16).reshape(TILES, TILE, BLK)
         xb[cb] = own
@@ -331,7 +338,7 @@
         y_start(yw0[k], k)
     send_in(xb, win0, 0, 0, TILES)
 
-    for c in loads[1:4]:
+    for c in loads[:3]:
         c.wait()
     for r in range(COLB):
         for k in range(2):
@@ -389,7 +396,6 @@
             yw1[9 + cb, tile : tile + tiles] = t.astype(jnp.bfloat16).reshape(tiles, TILE, BLK)
             tb[k][cb] = (t + 2.0 * b1).astype(jnp.bfloat16).reshape(tiles, TILE, BLK)
         send_in(tb[k], wint, 1, tile, tiles)
-    y_start(yw1, len(PARTS))
 
     a_table = class_table(acls)
     a_at = []
@@ -410,7 +416,7 @@
             slots.append(jnp.clip(slot, 0, 3))
         slot_at.append(slots)
 
-    for c in loads[4:]:
+    for c in loads[3:]:
         c.wait()
 
     @pl.when(is_home)
@@ -420,6 +426,8 @@
                 live = jnp.full((BLK, BLK), amask[k, a_block[j]].astype(jnp.float32))
                 aw[j, :, k * BLK : (k + 1) * BLK] = araw[j, k] * live.astype(jnp.bfloat16)
 
+
+    y_start(yw1, len(PARTS))
 
     @pl.when(is_home)
     def _():
@@ -486,6 +494,7 @@
             pltpu.VMEM((WIN, BLK, 2 * BLK), bf16),
             pltpu.VMEM((COLB, BLK, 2 * BLK), bf16),
             dma((8,)),
+            dma((TILES,)),
             *[dma((2, 4))] * 4,
             dma((1 + len(PARTS), 2, 4)),
             dma((4,)),

time: 31.4 us -> 31.4 us (level)
  no operation moved by 1% of the time
where the time goes in v8:
time: 31.4 us; the launch traced here: 31.3 us
  Pallas kernels  30.6 us (97%)
  between operations  0.64 us (2%)
    pallas_call x1, Pallas kernels, on_device(): pl.pallas_call(kernel, out_shape=[pltpu.VMEM((rows, columns), f32)] * 2,...  29.9 us
    pallas_call x1, Pallas kernels, on_device(): pl.pallas_call(hand_over, out_shape=[jax.ShapeDtypeStruct((rows, columns)...  0.73 us

profile of v8, /device:TPU:81, one launch (start us, length us, event | category | flops | bytes accessed | tf_op | source)
XLA Modules:
  0.0 31.3 jit_solution(1254567360057748997)
XLA Ops:
  0.6 29.9 %chebyshev_steps.1 = (f32[48,768]{1,0:T(8,128)S(1)}, f32[48,768]{1,0:T(8,128)S(1)}) custom-call(f32[48,768]{1,0:T(8,128)} %prev_hbm.1, f32[48,768]{1,0:T(8,128)} %this_hbm.1, f32[48,768]{1,0:T(8,128)} %diag_hbm.1, bf16[36,2,128,128]{3,2,1,0:T(8,128)(2,1)} %ablk_hbm.1, s32[8]{0:T(128)} %acls.1, s32[2,36]{1,0:T(2,128)} %bitcast.4, s32[2,36]{1,0:T(2,128)} %bitcast.5, ...), custom_call_target="tpu_custom_call" | custom-call | tf_op jit(solution)/shard_map/chebyshev_steps/pallas_call | solution.py:480
  30.5 0.7 %hand_over.1 = (f32[48,768]{1,0:T(8,128)}, f32[48,768]{1,0:T(8,128)}) custom-call(f32[48,768]{1,0:T(8,128)S(1)} %get-tuple-element.4.next_in, f32[48,768]{1,0:T(8,128)S(1)} %get-tuple-element.5.after_in), custom_call_target="tpu_custom_call" | custom-call | tf_op jit(solution)/shard_map/hand_over/pallas_call | solution.py:509
